TPU v7x, 32 devices: a whole 2x2x4 slice. The times are simulated.
32 devices in a mesh: dp: 8 (over y, x, core), mp: 4 (over z).
Axes of the slice: x: 2, y: 2, z: 4, core: 2. Of those that a mesh axis runs over, the one named last changes fastest.
Arguments:
- tokens: bfloat16 [6304, 768], P(('dp', 'mp')), may hold values from -6 to 6
- cotangent: bfloat16 [6304, 768], P(('dp', 'mp')), may hold values from -6 to 6
- ln1_gain: float32 [768], replicated, may hold values from 0.5 to 1.5
- ln1_bias: float32 [768], replicated, may hold values from -3 to 3
- w_query: bfloat16 [768, 768], P('dp', 'mp'), may hold values from -0.21875 to 0.21875
- query_bias: float32 [768], P('mp'), may hold values from -2 to 2
- w_key: bfloat16 [768, 768], P('dp', 'mp'), may hold values from -0.21875 to 0.21875
- w_value: bfloat16 [768, 768], P('dp', 'mp'), may hold values from -0.21875 to 0.21875
- value_bias: float32 [768], P('mp'), may hold values from -2 to 2
- w_out: bfloat16 [768, 768], P('dp', 'mp'), may hold values from -1.75 to 1.75
- out_bias: float32 [768], replicated, may hold values from -2 to 2
- ln2_gain: float32 [768], replicated, may hold values from 0.5 to 1.5
- ln2_bias: float32 [768], replicated, may hold values from -3 to 3
- w_up: bfloat16 [768, 3072], P('dp', 'mp'), may hold values from -0.21875 to 0.21875
- up_bias: float32 [3072], P('mp'), may hold values from -2 to 2
- w_down: bfloat16 [768, 3072], P('dp', 'mp'), may hold values from -0.109375 to 0.109375
- down_bias: float32 [768], replicated, may hold values from -2 to 2
Outputs:
- activations: bfloat16 [6304, 768], P(('dp', 'mp'))
- input_grad: float32 [6304, 768], P(('dp', 'mp'))
- ln1_gain_grad: float32 [768], replicated
- ln1_bias_grad: float32 [768], replicated
- w_query_grad: float32 [768, 768], P('dp', 'mp')
- query_bias_grad: float32 [768], P('mp')
- w_key_grad: float32 [768, 768], P('dp', 'mp')
- w_value_grad: float32 [768, 768], P('dp', 'mp')
- value_bias_grad: float32 [768], P('mp')
- w_out_grad: float32 [768, 768], P('dp', 'mp')
- out_bias_grad: float32 [768], replicated
- ln2_gain_grad: float32 [768], replicated
- ln2_bias_grad: float32 [768], replicated
- w_up_grad: float32 [768, 3072], P('dp', 'mp')
- up_bias_grad: float32 [3072], P('mp')
- w_down_grad: float32 [768, 3072], P('dp', 'mp')
- down_bias_grad: float32 [768], replicated
All inputs are finite; a program needn't handle non-finite values.
Results may differ from a plain program's by a relative error of at most 0.012.
Values may be sent and summed in bfloat16 or wider, within the bound.
A program may use at most 128 MiB of HBM per device.

v0:
```python
import jax
import jax.numpy as jnp
from jax import lax
from jax.sharding import PartitionSpec as P

HEAD_DIM = 64
SEQ = 197


norm_eps = 1e-06


def layer_norm(inputs, gain, shift):
    row_mean = jnp.mean(inputs, axis=-1, keepdims=True)
    centred = inputs - row_mean
    variance = jnp.mean(centred * centred, axis=-1, keepdims=True)
    return centred * lax.rsqrt(variance + norm_eps) * gain + shift


def gelu_exact(upper):
    return jax.nn.gelu(upper, approximate=False)


def matmul(left, right):
    return jnp.dot(left, right, preferred_element_type=jnp.float32)


def contract_rows(left, right):
    return lax.dot_general(
        left, right, (((0,), (0,)), ((), ())), preferred_element_type=jnp.float32
    )


def times_transposed(left, right):
    return lax.dot_general(
        left, right, (((1,), (1,)), ((), ())), preferred_element_type=jnp.float32
    )


def column_sums(grads_low):
    return jnp.sum(grads_low.astype(jnp.float32), axis=0)


def per_device(
    tokens,
    cotangent,
    ln1_gain,
    ln1_bias,
    w_query,
    query_bias,
    w_key,
    w_value,
    value_bias,
    w_out,
    out_bias,
    ln2_gain,
    ln2_bias,
    w_up,
    up_bias,
    w_down,
    down_bias,
):
    own_rows = tokens.shape[0]
    group_rows = own_rows * lax.axis_size("mp")
    images = group_rows // SEQ
    heads_local = w_query.shape[1] // HEAD_DIM
    scale = HEAD_DIM ** (-0.5)
    head_shape = (images, SEQ, heads_local, HEAD_DIM)
    owned = (w_query, w_key, w_value, w_out, w_up, w_down)
    fwd_query, fwd_key, fwd_value, fwd_out, fwd_up, fwd_down = (
        lax.all_gather(w_query, "dp", axis=0, tiled=True),
        lax.all_gather(w_key, "dp", axis=0, tiled=True),
        lax.all_gather(w_value, "dp", axis=0, tiled=True),
        lax.all_gather(w_out, "dp", axis=0, tiled=True),
        lax.all_gather(w_up, "dp", axis=0, tiled=True),
        lax.all_gather(w_down, "dp", axis=0, tiled=True),
    )
    inputs = tokens.astype(jnp.float32)
    normed, norm1_back = jax.vjp(layer_norm, inputs, ln1_gain, ln1_bias)
    group_normed = lax.all_gather(normed.astype(jnp.bfloat16), "mp", axis=0, tiled=True)
    queries = (
        (matmul(group_normed, fwd_query) + query_bias).astype(jnp.bfloat16).reshape(head_shape)
    )
    keys_low = matmul(group_normed, fwd_key).astype(jnp.bfloat16).reshape(head_shape)
    values_low = (
        (matmul(group_normed, fwd_value) + value_bias).astype(jnp.bfloat16).reshape(head_shape)
    )
    scaled = (
        jnp.einsum("bqhd,bkhd->bhqk", queries, keys_low, preferred_element_type=jnp.float32) * scale
    )
    row_top = jnp.max(scaled, axis=-1, keepdims=True)
    expos = jnp.exp(scaled - row_top)
    softmax_total = jnp.sum(expos, axis=-1, keepdims=True)
    log_total = row_top + jnp.log(softmax_total)
    probs_low = (expos / softmax_total).astype(jnp.bfloat16)
    mixed = jnp.einsum("bhqk,bkhd->bqhd", probs_low, values_low, preferred_element_type=jnp.float32)
    mixed = mixed.reshape(group_rows, heads_local * HEAD_DIM).astype(jnp.bfloat16)
    out_terms = times_transposed(mixed, fwd_out)
    middle = inputs + (
        lax.psum_scatter(out_terms, "mp", scatter_dimension=0, tiled=True) + out_bias
    )
    normed2, norm2_back = jax.vjp(layer_norm, middle, ln2_gain, ln2_bias)
    group_normed2 = lax.all_gather(normed2.astype(jnp.bfloat16), "mp", axis=0, tiled=True)
    upper = matmul(group_normed2, fwd_up) + up_bias
    hidden_f, gelu_back = jax.vjp(gelu_exact, upper)
    hidden = hidden_f.astype(jnp.bfloat16)
    down_terms = times_transposed(hidden, fwd_down)
    output = middle + (
        lax.psum_scatter(down_terms, "mp", scatter_dimension=0, tiled=True) + down_bias
    )
    activations = output.astype(jnp.bfloat16)
    back_query, back_key, back_value, back_out, back_up, back_down = (
        lax.all_gather(owned[0], "dp", axis=0, tiled=True),
        lax.all_gather(owned[1], "dp", axis=0, tiled=True),
        lax.all_gather(owned[2], "dp", axis=0, tiled=True),
        lax.all_gather(owned[3], "dp", axis=0, tiled=True),
        lax.all_gather(owned[4], "dp", axis=0, tiled=True),
        lax.all_gather(owned[5], "dp", axis=0, tiled=True),
    )
    grad_out = cotangent.astype(jnp.float32)
    grad_branch2 = grad_out.astype(jnp.bfloat16)
    down_bias_part = column_sums(grad_branch2)
    group_grad2 = lax.all_gather(grad_branch2, "mp", axis=0, tiled=True)
    w_down_part = contract_rows(group_grad2, hidden)
    grad_upper = gelu_back(matmul(group_grad2, back_down))[0].astype(jnp.bfloat16)
    up_bias_part = column_sums(grad_upper)
    w_up_part = contract_rows(group_normed2, grad_upper)
    up_terms = times_transposed(grad_upper, back_up)
    grad_normed2 = lax.psum_scatter(up_terms, "mp", scatter_dimension=0, tiled=True)
    grad_mid_norm, ln2_gain_part, ln2_bias_part = norm2_back(grad_normed2)
    grad_middle = grad_out + grad_mid_norm
    grad_branch = grad_middle.astype(jnp.bfloat16)
    out_bias_part = column_sums(grad_branch)
    group_grad1 = lax.all_gather(grad_branch, "mp", axis=0, tiled=True)
    w_out_part = contract_rows(group_grad1, mixed)
    grad_mixed = matmul(group_grad1, back_out).astype(jnp.bfloat16).reshape(head_shape)
    again = (
        jnp.einsum("bqhd,bkhd->bhqk", queries, keys_low, preferred_element_type=jnp.float32) * scale
    )
    probs = jnp.exp(again - log_total)
    probs_again = probs.astype(jnp.bfloat16)
    grad_probs = jnp.einsum(
        "bqhd,bkhd->bhqk", grad_mixed, values_low, preferred_element_type=jnp.float32
    )
    grad_values = jnp.einsum(
        "bhqk,bqhd->bkhd", probs_again, grad_mixed, preferred_element_type=jnp.float32
    )
    grad_values = grad_values.astype(jnp.bfloat16).reshape(group_rows, -1)
    inner = jnp.sum(probs * grad_probs, axis=-1, keepdims=True)
    grad_scores = (probs * (grad_probs - inner) * scale).astype(jnp.bfloat16)
    grad_queries = jnp.einsum(
        "bhqk,bkhd->bqhd", grad_scores, keys_low, preferred_element_type=jnp.float32
    )
    grad_queries = grad_queries.astype(jnp.bfloat16).reshape(group_rows, -1)
    grad_keys = jnp.einsum(
        "bhqk,bqhd->bkhd", grad_scores, queries, preferred_element_type=jnp.float32
    )
    grad_keys = grad_keys.astype(jnp.bfloat16).reshape(group_rows, -1)
    query_bias_part = column_sums(grad_queries)
    value_bias_part = column_sums(grad_values)
    w_query_part = contract_rows(group_normed, grad_queries)
    w_key_part = contract_rows(group_normed, grad_keys)
    w_value_part = contract_rows(group_normed, grad_values)
    qkv_terms = times_transposed(grad_queries, back_query)
    qkv_terms = qkv_terms + times_transposed(grad_keys, back_key)
    qkv_terms = qkv_terms + times_transposed(grad_values, back_value)
    grad_normed = lax.psum_scatter(qkv_terms, "mp", scatter_dimension=0, tiled=True)
    grad_in_norm, ln1_gain_part, ln1_bias_part = norm1_back(grad_normed)
    input_grad = grad_middle + grad_in_norm
    w_query_grad, w_key_grad, w_value_grad, w_out_grad, w_up_grad, w_down_grad = (
        lax.psum_scatter(w_query_part, "dp", scatter_dimension=0, tiled=True),
        lax.psum_scatter(w_key_part, "dp", scatter_dimension=0, tiled=True),
        lax.psum_scatter(w_value_part, "dp", scatter_dimension=0, tiled=True),
        lax.psum_scatter(w_out_part, "dp", scatter_dimension=0, tiled=True),
        lax.psum_scatter(w_up_part, "dp", scatter_dimension=0, tiled=True),
        lax.psum_scatter(w_down_part, "dp", scatter_dimension=0, tiled=True),
    )
    ln1_gain_grad, ln1_bias_grad, out_bias_grad, ln2_gain_grad, ln2_bias_grad, down_bias_grad = (
        lax.psum(
            (
                ln1_gain_part,
                ln1_bias_part,
                out_bias_part,
                ln2_gain_part,
                ln2_bias_part,
                down_bias_part,
            ),
            ("dp", "mp"),
        )
    )
    query_bias_grad, value_bias_grad, up_bias_grad = lax.psum(
        (query_bias_part, value_bias_part, up_bias_part), "dp"
    )
    return (
        activations,
        input_grad,
        ln1_gain_grad,
        ln1_bias_grad,
        w_query_grad,
        query_bias_grad,
        w_key_grad,
        w_value_grad,
        value_bias_grad,
        w_out_grad,
        out_bias_grad,
        ln2_gain_grad,
        ln2_bias_grad,
        w_up_grad,
        up_bias_grad,
        w_down_grad,
        down_bias_grad,
    )


def solution(mesh):
    in_specs = (
        P(("dp", "mp"), None),
        P(("dp", "mp"), None),
        P(),
        P(),
        P("dp", "mp"),
        P("mp"),
        P("dp", "mp"),
        P("dp", "mp"),
        P("mp"),
        P("dp", "mp"),
        P(),
        P(),
        P(),
        P("dp", "mp"),
        P("mp"),
        P("dp", "mp"),
        P(),
    )
    out_specs = (
        P(("dp", "mp"), None),
        P(("dp", "mp"), None),
        P(),
        P(),
        P("dp", "mp"),
        P("mp"),
        P("dp", "mp"),
        P("dp", "mp"),
        P("mp"),
        P("dp", "mp"),
        P(),
        P(),
        P(),
        P("dp", "mp"),
        P("mp"),
        P("dp", "mp"),
        P(),
    )
    return jax.shard_map(
        per_device, mesh=mesh, in_specs=in_specs, out_specs=out_specs, check_vma=False
    )
```

profile of v0, /device:TPU:0, one launch (start us, length us, event | category | flops | bytes accessed | tf_op | source)
XLA Modules:
  0.0 562.4 jit_solution(3668613329379731804)
XLA Ops:
  12.3 11.3 %all_gather.38 = bf16[768,192]{1,0:T(8,128)(2,1)S(1)} all-gather(bf16[96,192]{1,0:T(8,128)(2,1)} %param.21), channel_id=1, replica_groups=mesh['dp'=8,'mp'=4] {'dp'}, dimensions={0}, use_global_device_ids=true | all-gather | bytes 331776 | tf_op jit(solution)/shard_map/all_gather | solution.py:71
  23.6 9.3 %all_gather.39 = bf16[768,192]{1,0:T(8,128)(2,1)S(1)} all-gather(bf16[96,192]{1,0:T(8,128)(2,1)} %param.23), channel_id=1, replica_groups=mesh['dp'=8,'mp'=4] {'dp'}, dimensions={0}, use_global_device_ids=true | all-gather | bytes 331776 | tf_op jit(solution)/shard_map/all_gather | solution.py:72
  32.9 8.9 %all_gather.37 = bf16[768,192]{1,0:T(8,128)(2,1)S(1)} all-gather(bf16[96,192]{1,0:T(8,128)(2,1)S(1)} %copy-done.26), channel_id=1, replica_groups=mesh['dp'=8,'mp'=4] {'dp'}, dimensions={0}, use_global_device_ids=true | all-gather | bytes 331776 | tf_op jit(solution)/shard_map/all_gather | solution.py:73
  41.8 9.3 %all_gather.40 = bf16[768,192]{1,0:T(8,128)(2,1)S(1)} all-gather(bf16[96,192]{1,0:T(8,128)(2,1)S(1)} %copy-done.27), channel_id=1, replica_groups=mesh['dp'=8,'mp'=4] {'dp'}, dimensions={0}, use_global_device_ids=true | all-gather | bytes 331776 | tf_op jit(solution)/shard_map/all_gather | solution.py:74
  62.9 54.9 %fusion = f32[200,768]{1,0:T(8,128)S(1)} fusion(f32[788,768]{1,0:T(8,128)} %fusion.86), kind=kCustom, calls=%all-reduce-scatter | all-reduce-scatter fusion | flops 614401 | bytes 3035648
  126.9 28.4 %all-gather.17.cloned.1.call-done = bf16[4,197,768]{2,1,0:T(8,128)(2,1)} async-done(((bf16[1,197,768]{2,1,0:T(8,128)(2,1)}), bf16[4,197,768]{2,1,0:T(8,128)(2,1)}) %all-gather.17.cloned.1.call-update) | async-done | bytes 1210384 | tf_op jit(solution)/shard_map/all_gather | solution.py:103
  156.9 23.3 %all-gather.11.cloned.1.call-done = bf16[768,768]{1,0:T(8,128)(2,1)} async-done(((bf16[96,768]{1,0:T(8,128)(2,1)}), bf16[768,768]{1,0:T(8,128)(2,1)}) %all-gather.11.cloned.1.call-update) | async-done | bytes 1179664 | tf_op jit(solution)/shard_map/all_gather | solution.py:75
  180.2 3.9 fusion.87
  184.0 21.9 %all-gather.13.cloned.1.call-done = bf16[768,768]{1,0:T(8,128)(2,1)} async-done(((bf16[96,768]{1,0:T(8,128)(2,1)}), bf16[768,768]{1,0:T(8,128)(2,1)}) %all-gather.13.cloned.1.call-update) | async-done | bytes 1179664 | tf_op jit(solution)/shard_map/all_gather | solution.py:76
  206.0 9.9 %convert_reduce_fusion = (f32[768]{0:T(1024)S(1)}, bf16[788,768]{1,0:T(8,128)(2,1)S(1)}, f32[788,768]{1,0:T(8,128)}) fusion(f32[788,768]{1,0:T(8,128)} %fusion.87, f32[768]{0:T(1024)S(1)} %copy-done.31, bf16[788,768]{1,0:T(8,128)(2,1)} %reshape.151, bf16[768,768]{1,0:T(8,128)(2,1)} %all-gather.13.cloned.1.call-done), kind=kOutput, calls=%fused_computation.9 | convolution fusion | flops 974950656 | bytes 8448000 | tf_op jit(solution)/shard_map/dot_general | solution.py:25
  219.5 49.6 %fusion.2 = f32[200,768]{1,0:T(8,128)S(1)} fusion(f32[788,768]{1,0:T(8,128)} %fusion.89), kind=kCustom, calls=%all-reduce-scatter.2 | all-reduce-scatter fusion | flops 614401 | bytes 3035648
  276.9 30.6 %all-gather.21.cloned.1.call-done = bf16[4,197,768]{2,1,0:T(8,128)(2,1)} async-done(((bf16[1,197,768]{2,1,0:T(8,128)(2,1)}), bf16[4,197,768]{2,1,0:T(8,128)(2,1)}) %all-gather.21.cloned.1.call-update) | async-done | bytes 1210384 | tf_op jit(solution)/shard_map/all_gather | solution.py:134
  320.2 3.0 fusion.57
  323.2 5.1 fusion.33
  332.3 6.0 %convert_reduce_fusion.3 = (f32[3,64]{1,0:T(4,128)S(1)}, bf16[4,197,3,64]{1,3,2,0:T(8,128)(2,1)}) fusion(f32[4,3,197,197]{2,3,1,0:T(8,128)} %fusion.57, f32[4,3,197]{2,1,0:T(4,128)S(1)} %log_add_fusion, f32[4,3,197,197]{2,3,1,0:T(8,128)} %copy-done, bf16[4,197,3,64]{1,0,3,2:T(4,128)(2,1)S(1)} %copy-done.18), kind=kOutput, calls=%fused_computation.58 | convolution fusion | flops 64258252 | bytes 4341072 | tf_op jit(solution)/shard_map/bhqk,bkhd->bqhd/dot_general | solution.py:151
  346.2 2.9 convolution_bitcast_fusion
  349.1 3.1 copy.85
  352.3 4.6 fusion.96
  356.9 4.3 fusion.88
  364.8 86.1 %fusion.79 = (f32[200,768]{1,0:T(8,128)S(1)}, f32[200,768]{1,0:T(8,128)S(1)}) fusion(f32[788,768]{1,0:T(8,128)} %fusion.88, f32[788,768]{1,0:T(8,128)} %add_add_fusion), kind=kCustom, calls=%all-reduce-scatter.4 | all-reduce-scatter fusion | flops 1228801 | bytes 6070784
  456.0 13.4 %all-reduce.9 = (f32[192]{0:T(256)}, f32[192]{0:T(256)}, f32[768]{0:T(1024)}) all-reduce(f32[192]{0:T(256)S(1)} %reduce_sum.220, f32[192]{0:T(256)S(1)} %reduce_sum.222, f32[768]{0:T(1024)S(1)} %get-tuple-element.87), channel_id=1, replica_groups=mesh['dp'=8,'mp'=4] {'dp'}, use_global_device_ids=true, to_apply=%region_21.0 | all-reduce | flops 1152 | bytes 9216 | tf_op jit(solution)/shard_map/psum | solution.py:191
  471.6 2.9 concatenate.1
  476.4 38.7 %all-reduce.8 = (f32[768]{0:T(1024)}, f32[768]{0:T(1024)}, f32[768]{0:T(1024)}, f32[768]{0:T(1024)}, f32[768]{0:T(1024)}, /*index=5*/f32[768]{0:T(1024)}) all-reduce(f32[768]{0:T(1024)S(1)} %get-tuple-element.70, f32[768]{0:T(1024)S(1)} %get-tuple-element.73, ...), channel_id=1, replica_groups=mesh['dp'=8,'mp'=4] {'dp','mp'}, use_global_device_ids=true, to_apply=%region_16.0 | all-reduce | flops 4608 | bytes 36864 | tf_op jit(solution)/shard_map/psum | solution.py:179
  516.0 39.1 %reduce-scatter.25.cloned.1.call-done = f32[96,768]{1,0:T(8,128)} async-done(((f32[768,768]{1,0:T(8,128)}), f32[96,768]{1,0:T(8,128)}) %reduce-scatter.25.cloned.1.call-update) | async-done | bytes 294928 | tf_op jit(solution)/shard_map/reduce_scatter | solution.py:175
  (181 shorter events, 76.0 us)
Async XLA Ops:
  7.2 34.6 %copy-start.27 = (bf16[96,192]{1,0:T(8,128)(2,1)S(1)}, bf16[96,192]{1,0:T(8,128)(2,1)}, u32[]{:S(2)}) copy-start(bf16[96,192]{1,0:T(8,128)(2,1)} %param.26) | copy-start | bytes 110596
  7.2 43.9 %all-gather.15.cloned.1.call-start = ((), (), s32[]{:S(2)}) async-start(), calls=%async_computation.13 | async-start | bytes 1536000 | tf_op jit(solution)/shard_map/all_gather | solution.py:80
  11.5 41.4 %copy-start.35 = (f32[192]{0:T(256)S(1)}, f32[192]{0:T(256)}, u32[]{:S(2)}) copy-start(f32[192]{0:T(256)} %param.22) | copy-start | bytes 2308
  11.5 112.6 %all-gather.19.cloned.1.call-start = ((), (), s32[]{:S(2)}) async-start(), calls=%async_computation.15 | async-start | bytes 1536000 | tf_op jit(solution)/shard_map/all_gather | solution.py:123
  12.3 143.0 %all-gather.17.cloned.1.call-start = ((), (), s32[]{:S(2)}) async-start(), calls=%async_computation.14 | async-start | bytes 1536000 | tf_op jit(solution)/shard_map/all_gather | solution.py:103
  60.9 58.2 %copy-start.33 = (u32[32]{0:T(128)S(1)}, u32[32]{0:T(128)}, u32[]{:S(2)}) copy-start(u32[32]{0:T(128)} %constant.85) | copy-start | bytes 388
  62.9 58.4 %copy-start.1 = (bf16[197,768]{1,0:T(8,128)(2,1)S(1)}, bf16[197,768]{1,0:T(8,128)(2,1)}, u32[]{:S(2)}) copy-start(bf16[197,768]{1,0:T(8,128)(2,1)} %param.17) | copy-start | bytes 907780
  62.9 58.4 %copy-start.29 = (f32[768]{0:T(1024)S(1)}, f32[768]{0:T(1024)}, u32[]{:S(2)}) copy-start(f32[768]{0:T(1024)} %param.27) | copy-start | bytes 9220
  117.8 3.0 collective-permute-start
  122.7 57.4 %all-gather.11.cloned.1.call-start = ((), (), s32[]{:S(2)}) async-start(), calls=%async_computation.6 | async-start | bytes 1327104 | tf_op jit(solution)/shard_map/all_gather | solution.py:75
  123.3 82.7 %all-gather.13.cloned.1.call-start = ((), (), s32[]{:S(2)}) async-start(), calls=%async_computation.7 | async-start | bytes 1327104 | tf_op jit(solution)/shard_map/all_gather | solution.py:76
  123.9 183.5 %all-gather.21.cloned.1.call-start = ((), (), s32[]{:S(2)}) async-start(), calls=%async_computation.16 | async-start | bytes 1536000 | tf_op jit(solution)/shard_map/all_gather | solution.py:134
  156.9 49.1 %copy-start.31 = (f32[768]{0:T(1024)S(1)}, f32[768]{0:T(1024)}, u32[]{:S(2)}) copy-start(f32[768]{0:T(1024)} %param.31) | copy-start | bytes 9220
  269.1 3.2 collective-permute-start.2
  276.8 239.1 %reduce-scatter.23.cloned.1.call-start = ((), (), s32[]{:S(2)}) async-start(), calls=%async_computation.11 | async-start | bytes 884736 | tf_op jit(solution)/shard_map/reduce_scatter | solution.py:174
  311.6 204.4 %reduce-scatter.21.cloned.1.call-start = ((), (), s32[]{:S(2)}) async-start(), calls=%async_computation.10 | async-start | bytes 884736 | tf_op jit(solution)/shard_map/reduce_scatter | solution.py:173
  319.9 196.0 %reduce-scatter.19.cloned.1.call-start = ((), (), s32[]{:S(2)}) async-start(), calls=%async_computation.9 | async-start | bytes 884736 | tf_op jit(solution)/shard_map/reduce_scatter | solution.py:172
  332.3 183.7 %reduce-scatter.17.cloned.1.call-start = ((), (), s32[]{:S(2)}) async-start(), calls=%async_computation.8 | async-start | bytes 884736 | tf_op jit(solution)/shard_map/reduce_scatter | solution.py:171
  343.3 172.7 %reduce-scatter.27.cloned.1.call-start = ((), (), s32[]{:S(2)}) async-start(), calls=%async_computation.17 | async-start | bytes 2654208
  352.2 202.9 %reduce-scatter.25.cloned.1.call-start = ((), (), s32[]{:S(2)}) async-start(), calls=%async_computation.12 | async-start | bytes 2654208 | tf_op jit(solution)/shard_map/reduce_scatter | solution.py:175
  451.0 18.4 %collective-permute-start.3 = (f32[9,768]{1,0:T(8,128)S(1)}, f32[9,768]{1,0:T(8,128)S(1)}, u32[]{:S(2)}, u32[]{:S(2)}) collective-permute-start(f32[9,768]{1,0:T(8,128)S(1)} %slice.3), channel_id=1, source_target_pairs={{0,1},{1,2},{2,3},{4,5},{5,6},{6,7},{8,9},{9,10},{10,11},{12,13},{... | collective-permute-start | bytes 82952
  453.4 18.1 %collective-permute-start.1 = (f32[9,768]{1,0:T(8,128)S(1)}, f32[9,768]{1,0:T(8,128)S(1)}, u32[]{:S(2)}, u32[]{:S(2)}) collective-permute-start(f32[9,768]{1,0:T(8,128)S(1)} %slice.1), channel_id=1, source_target_pairs={{0,1},{1,2},{2,3},{4,5},{5,6},{6,7},{8,9},{9,10},{10,11},{12,13},{... | collective-permute-start | bytes 82952
  474.5 40.6 %copy-start.12 = (f32[209,768]{1,0:T(8,128)S(1)}, f32[209,768]{1,0:T(8,128)}, u32[]{:S(2)}) copy-start(f32[209,768]{1,0:T(8,128)} %concatenate.1) | copy-start | bytes 1926148
  474.5 40.6 %copy-start.32 = (f32[768]{0:T(1024)S(1)}, f32[768]{0:T(1024)}, u32[]{:S(2)}) copy-start(f32[768]{0:T(1024)} %param.33) | copy-start | bytes 9220
  (30 other events, 279.9 us)
Sparse Core Ops, SparseCore 0:
  11.6 33.9 all-gather.14
  47.2 36.6 all-gather.18
  122.9 32.3 all-gather.16
  157.0 23.1 all-gather.10
  181.9 24.0 all-gather.12
  276.9 30.4 all-gather.20
  311.7 34.1 reduce-scatter.22
  349.6 34.9 reduce-scatter.20
  388.3 34.9 reduce-scatter.18
  426.9 35.0 reduce-scatter.16
  465.9 42.5 reduce-scatter.26
  512.6 42.4 reduce-scatter.24
where the time goes:
time: 571 us; the launch traced here: 562 us
  blocking collectives  281 us (49%)
  waiting for transfers between devices  147 us (26%)
  matrix products  63.1 us (11%)
  local copies, waits for them, and re-layouts  32.8 us (6%)
  between operations  16 us (3%)
  other arithmetic  13.2 us (2%)
  starting transfers between devices  8.36 us (1%)
    unnamed x3, blocking collectives  191 us
    reduce_scatter x1, waiting for transfers between devices, per_device(): lax.psum_scatter(w_up_part, 'dp', scatter_dimension=0, tiled=True)  39.1 us
    psum x1, blocking collectives, per_device(): lax.psum((ln1_gain_part, ln1_bias_part, out_bias_part, ln2_gain_part, ln2...  38.7 us
    all_gather x1, waiting for transfers between devices, per_device(): group_grad1 = lax.all_gather(grad_branch, 'mp', axis=0, tiled=True)  30.6 us
    all_gather x1, waiting for transfers between devices, per_device(): lax.all_gather(normed2.astype(jnp.bfloat16), 'mp', axis=0, tiled=True)  28.4 us
    all_gather x1, waiting for transfers between devices, per_device(): lax.all_gather(w_up, 'dp', axis=0, tiled=True)  23.3 us
    unnamed x90, local copies, waits for them, and re-layouts  22.3 us
    all_gather x1, waiting for transfers between devices, per_device(): lax.all_gather(w_down, 'dp', axis=0, tiled=True)  21.9 us
  transfers between devices with their start and end apart: 16, of which 7 were waited for; matrix products, arithmetic and copies ran while one was open for 40% of the time, Pallas kernels for 0%

commit v1 on v0

v1 whole, which is shorter than its diff:
```python
import functools

import jax
import jax.numpy as jnp
from jax import lax
from jax.experimental import pallas as pl
from jax.experimental.pallas import tpu as pltpu
from jax.sharding import PartitionSpec as P

HEAD_DIM = 64
SEQ = 197
MESH = pl.DeviceIdType.MESH

norm_eps = 1e-06


def layer_norm(inputs, gain, shift):
    row_mean = jnp.mean(inputs, axis=-1, keepdims=True)
    centred = inputs - row_mean
    variance = jnp.mean(centred * centred, axis=-1, keepdims=True)
    return centred * lax.rsqrt(variance + norm_eps) * gain + shift


def gelu_exact(upper):
    return jax.nn.gelu(upper, approximate=False)


def matmul(left, right):
    return jnp.dot(left, right, preferred_element_type=jnp.float32)


def contract_rows(left, right):
    return lax.dot_general(
        left, right, (((0,), (0,)), ((), ())), preferred_element_type=jnp.float32
    )


def times_transposed(left, right):
    return lax.dot_general(
        left, right, (((1,), (1,)), ((), ())), preferred_element_type=jnp.float32
    )


def column_sums(grads_low):
    return jnp.sum(grads_low.astype(jnp.float32), axis=0)


def flip(index, bit):
    return index + (1 << bit) * (1 - 2 * bit_of(index, bit))


def bit_of(index, bit):
    return lax.rem(lax.div(index, 1 << bit), 2)


def bits_in(size):
    return size.bit_length() - 1


def dp_order(n_bits, variant):
    rest = list(range(1, n_bits))
    if variant:
        rest = rest[::-1]
    return [0] + rest if n_bits else []


def greet(dp, mp, dp_bits, mp_bits):
    barrier = pltpu.get_barrier_semaphore()
    for bit in range(dp_bits):
        pl.semaphore_signal(barrier, inc=1, device_id=(flip(dp, bit), mp), device_id_type=MESH)
    for bit in range(mp_bits):
        pl.semaphore_signal(barrier, inc=1, device_id=(dp, flip(mp, bit)), device_id_type=MESH)
    pl.semaphore_wait(barrier, dp_bits + mp_bits)


def gather_plan(dp_bits, mp_bits, variant):
    stages = []
    done_mp = []
    for bit in range(mp_bits)[::-1]:
        stages.append(("mp", bit, (), tuple(done_mp)))
        done_mp.append(bit)
    done_dp = []
    for bit in dp_order(dp_bits, variant)[::-1]:
        stages.append(("dp", bit, tuple(done_dp), tuple(done_mp)))
        done_dp.append(bit)
    return stages


def subsets(index, handled):
    out = [index]
    for bit in handled:
        out = out + [flip(item, bit) for item in out]
    return out


def gather_kernel(n_dp, n_mp, halves, n_mats, *refs):
    shards, outs = refs[:n_mats], refs[n_mats : 2 * n_mats]
    send_sem, recv_sem, own_sem = refs[2 * n_mats :]
    dp_bits, mp_bits = bits_in(n_dp), bits_in(n_mp)
    rows, width = shards[0].shape
    piece = rows // halves
    dp, mp = lax.axis_index("dp"), lax.axis_index("mp")

    def columns(m):
        return pl.ds(pl.multiple_of(m * width, width), width)

    def part(mat, half, d, m):
        row = pl.ds(half * piece, piece)
        if m is None:
            return outs[mat].at[d, row, :]
        return outs[mat].at[d, row, columns(m)]

    locals_ = []
    for mat in range(n_mats):
        copy = pltpu.make_async_copy(
            shards[mat], outs[mat].at[dp, :, columns(mp)], own_sem.at[mat]
        )
        copy.start()
        locals_.append(copy)
    greet(dp, mp, dp_bits, mp_bits)
    for copy in locals_:
        copy.wait()

    sent = []
    waiting = {}
    n_stages = dp_bits + mp_bits

    def run(mat, half, stage):
        variant = half if halves > 1 else mat % 2
        chunk = mat * halves + half
        axis, bit, done_dp, done_mp = gather_plan(dp_bits, mp_bits, variant)[stage]
        if axis == "mp":
            mine = [(dp, m) for m in subsets(mp, done_mp)]
            theirs = [(dp, m) for m in subsets(flip(mp, bit), done_mp)]
            target = (dp, flip(mp, bit))
        else:
            mine = [(d, None) for d in subsets(dp, done_dp)]
            theirs = [(d, None) for d in subsets(flip(dp, bit), done_dp)]
            target = (flip(dp, bit), mp)
        slot = 0
        for earlier in range(stage):
            _, _, e_dp, e_mp = gather_plan(dp_bits, mp_bits, variant)[earlier]
            slot += 1 << (len(e_mp) if earlier < mp_bits else len(e_dp))
        for number, ((d, m), (their_d, their_m)) in enumerate(zip(mine, theirs)):
            sems = dict(
                send_sem=send_sem.at[chunk, slot + number],
                recv_sem=recv_sem.at[chunk, slot + number],
                device_id=target,
                device_id_type=MESH,
            )
            source = part(mat, half, d, m)
            copy = pltpu.make_async_remote_copy(src_ref=source, dst_ref=source, **sems)
            copy.start()
            sent.append(copy)
            landing = part(mat, half, their_d, their_m)
            waiting.setdefault((mat, half), []).append(
                pltpu.make_async_remote_copy(src_ref=landing, dst_ref=landing, **sems)
            )

    def settle(mat, half):
        for copy in waiting.pop((mat, half), []):
            copy.wait_recv()

    for step in range(n_mats + n_stages):
        for stage in range(n_stages + 1)[::-1]:
            mat = step - stage
            if 0 <= mat < n_mats:
                for half in range(halves):
                    settle(mat, half)
                    if stage < n_stages:
                        run(mat, half, stage)
    for copy in sent:
        copy.wait_send()


def gather_weights(shards, n_dp, n_mp):
    rows, width = shards[0].shape
    n_mats = len(shards)
    halves = 2 if rows % 32 == 0 else 1
    copies = (n_mp - 1) + (n_dp - 1)
    return pl.pallas_call(
        functools.partial(gather_kernel, n_dp, n_mp, halves, n_mats),
        out_shape=[jax.ShapeDtypeStruct((n_dp, rows, n_mp * width), jnp.bfloat16)] * n_mats,
        in_specs=[pl.BlockSpec(memory_space=pl.ANY)] * n_mats,
        out_specs=[pl.BlockSpec(memory_space=pl.ANY)] * n_mats,
        scratch_shapes=[
            pltpu.SemaphoreType.DMA((n_mats * halves, copies)),
            pltpu.SemaphoreType.DMA((n_mats * halves, copies)),
            pltpu.SemaphoreType.DMA((n_mats,)),
        ],
        compiler_params=pltpu.CompilerParams(collective_id=0, has_side_effects=True),
    )(*shards)


def reduce_kernel(n_dp, n_mp, halves, n_mats, *refs):
    parts, vectors = refs[:n_mats], refs[n_mats]
    sums, vector_sum = refs[n_mats + 1 : n_mats + 3]
    dp_bits, mp_bits = bits_in(n_dp), bits_in(n_mp)
    n_stages = dp_bits + mp_bits
    scratch = refs[n_mats + 3 :]
    kept = scratch[0]
    landed = scratch[1 : 1 + n_stages]
    vector_in = scratch[1 + n_stages]
    vector_at = scratch[2 + n_stages]
    send_sem, recv_sem, kept_sem, v_send, v_recv = scratch[3 + n_stages :]
    rows = sums.shape[1]
    width = sums.shape[2]
    piece = rows // halves
    group = 16 if piece % 16 == 0 else piece
    dp, mp = lax.axis_index("dp"), lax.axis_index("mp")

    def arranged(order, fixed_bit, value):
        out = [value * (1 << fixed_bit)]
        for bit in order:
            out = [item + (side << bit) for item in out for side in (0, 1)]
        return out

    greet(dp, mp, dp_bits, mp_bits)
    vector_at[0] = vectors[...]
    sent = []
    waiting = {}
    vector_wait = []

    def partner(axis, bit):
        if axis == "dp":
            return (flip(dp, bit), mp)
        return (dp, flip(mp, bit))

    def stages_of(variant):
        order = dp_order(dp_bits, variant)
        return [("dp", bit) for bit in order] + [("mp", bit) for bit in range(mp_bits)]

    def send(key, source, landing, sem, target):
        copy = pltpu.make_async_remote_copy(
            src_ref=source,
            dst_ref=landing,
            send_sem=send_sem.at[sem],
            recv_sem=recv_sem.at[sem],
            device_id=target,
            device_id_type=MESH,
        )
        copy.start()
        sent.append(copy)
        waiting.setdefault(key, []).append(copy)

    first = n_dp // 2

    def run(mat, half, stage):
        variant = half if halves > 1 else mat % 2
        chunk = mat * halves + half
        plan = stages_of(variant)
        axis, bit = plan[stage]
        target = partner(axis, bit)
        key = (mat, half)
        row = pl.ds(half * piece, piece)
        if stage == 0:
            order = [b for _, b in plan[1:dp_bits]]
            side = bit_of(dp, bit)
            for number, block in enumerate(arranged(order, bit, 1 - side)):
                send(
                    key,
                    parts[mat].at[block, row, :],
                    landed[0].at[chunk, number],
                    (chunk, number),
                    target,
                )
            for number, block in enumerate(arranged(order, bit, side)):
                copy = pltpu.make_async_copy(
                    parts[mat].at[block, row, :], kept.at[chunk, number], kept_sem.at[chunk, number]
                )
                copy.start()
                waiting[key].append(copy)
        elif axis == "dp":
            count = n_dp >> (stage + 1)
            start = (1 - bit_of(dp, bit)) * count
            send(
                key,
                landed[stage - 1].at[chunk, pl.ds(start, count)],
                landed[stage].at[chunk],
                (chunk, first + stage - 1),
                target,
            )
        else:
            count = n_mp >> (bit + 1)
            slot = first + dp_bits - 1 + (n_mp - (n_mp >> bit))
            for number in range(count):
                block = 2 * number + 1 - bit_of(mp, bit)
                send(
                    key,
                    landed[stage - 1].at[chunk, 0, :, pl.ds(pl.multiple_of(block * width, width), width)],
                    landed[stage].at[chunk, 0, :, pl.ds(number * width, width)],
                    (chunk, slot + number),
                    target,
                )

    def settle(mat, half, stage):
        variant = half if halves > 1 else mat % 2
        chunk = mat * halves + half
        for copy in waiting.pop((mat, half)):
            if hasattr(copy, "wait_recv") and copy.is_remote:
                copy.wait_recv()
            else:
                copy.wait()
        axis, bit = stages_of(variant)[stage]
        last = stage == n_stages - 1
        into = landed[stage]
        blocks = into.shape[1]

        @pl.loop(0, blocks * (piece // group))
        def _(at):
            block = lax.div(at, piece // group)
            start = lax.rem(at, piece // group) * group
            if group % 16 == 0:
                start = pl.multiple_of(start, group)
            here = pl.ds(start, group)
            if axis == "dp":
                if stage == 0:
                    own = kept[chunk, block, here, :]
                else:
                    base = bit_of(dp, bit) * blocks
                    own = landed[stage - 1][chunk, base + block, here, :]
                total = own.astype(jnp.float32) + into[chunk, block, here, :].astype(jnp.float32)
                into[chunk, block, here, :] = total.astype(jnp.bfloat16)
            else:
                for number in range(n_mp >> (bit + 1)):
                    source = 2 * number + bit_of(mp, bit)
                    own = landed[stage - 1][
                        chunk, 0, here, pl.ds(pl.multiple_of(source * width, width), width)
                    ]
                    cols = pl.ds(number * width, width)
                    total = own.astype(jnp.float32) + into[chunk, 0, here, cols].astype(jnp.float32)
                    if last:
                        place = pl.ds(half * piece + start, group)
                        sums[mat, place, :] = total
                    else:
                        into[chunk, 0, here, cols] = total.astype(jnp.bfloat16)

    vector_plan = stages_of(0)

    def vector_send(stage):
        axis, bit = vector_plan[stage]
        copy = pltpu.make_async_remote_copy(
            src_ref=vector_at.at[stage],
            dst_ref=vector_in.at[stage],
            send_sem=v_send.at[stage],
            recv_sem=v_recv.at[stage],
            device_id=partner(axis, bit),
            device_id_type=MESH,
        )
        copy.start()
        vector_wait.append(copy)

    def vector_settle(stage):
        vector_wait[stage].wait()
        total = vector_at[stage] + vector_in[stage]
        if stage == n_stages - 1:
            vector_sum[...] = total
        else:
            vector_at[stage + 1] = total

    for step in range(n_mats + n_stages):
        if 1 <= step <= n_stages:
            vector_settle(step - 1)
        if step < n_stages:
            vector_send(step)
        for stage in range(n_stages + 1)[::-1]:
            mat = step - stage
            if 0 <= mat < n_mats:
                for half in range(halves):
                    if stage > 0:
                        settle(mat, half, stage - 1)
                    if stage < n_stages:
                        run(mat, half, stage)
    for copy in sent:
        copy.wait_send()


def reduce_gradients(parts, vectors, n_dp, n_mp):
    n_mats = len(parts)
    _, rows, full = parts[0].shape
    width = full // n_mp
    halves = 2 if rows % 32 == 0 else 1
    piece = rows // halves
    chunks = n_mats * halves
    dp_bits, mp_bits = bits_in(n_dp), bits_in(n_mp)
    n_stages = dp_bits + mp_bits
    landings = [
        pltpu.VMEM((chunks, n_dp >> (stage + 1), piece, full), jnp.bfloat16)
        for stage in range(dp_bits)
    ] + [
        pltpu.VMEM((chunks, 1, piece, full >> (stage + 1)), jnp.bfloat16)
        for stage in range(mp_bits)
    ]
    copies = n_dp // 2 + dp_bits - 1 + n_mp - 1
    return pl.pallas_call(
        functools.partial(reduce_kernel, n_dp, n_mp, halves, n_mats),
        out_shape=[
            jax.ShapeDtypeStruct((n_mats, rows, width), jnp.float32),
            jax.ShapeDtypeStruct(vectors.shape, jnp.float32),
        ],
        in_specs=[pl.BlockSpec(memory_space=pl.ANY)] * n_mats
        + [pl.BlockSpec(memory_space=pltpu.VMEM)],
        out_specs=[pl.BlockSpec(memory_space=pltpu.VMEM)] * 2,
        scratch_shapes=[
            pltpu.VMEM((chunks, n_dp // 2, piece, full), jnp.bfloat16),
            *landings,
            pltpu.VMEM((n_stages,) + vectors.shape, jnp.float32),
            pltpu.VMEM((n_stages,) + vectors.shape, jnp.float32),
            pltpu.SemaphoreType.DMA((chunks, copies)),
            pltpu.SemaphoreType.DMA((chunks, copies)),
            pltpu.SemaphoreType.DMA((chunks, n_dp // 2)),
            pltpu.SemaphoreType.DMA((n_stages,)),
            pltpu.SemaphoreType.DMA((n_stages,)),
        ],
        compiler_params=pltpu.CompilerParams(
            collective_id=1, has_side_effects=True, vmem_limit_bytes=48 * 1024 * 1024
        ),
    )(*parts, vectors)


def per_device(
    n_dp,
    n_mp,
    tokens,
    cotangent,
    ln1_gain,
    ln1_bias,
    w_query,
    query_bias,
    w_key,
    w_value,
    value_bias,
    w_out,
    out_bias,
    ln2_gain,
    ln2_bias,
    w_up,
    up_bias,
    w_down,
    down_bias,
):
    own_rows, width = tokens.shape
    images = own_rows // SEQ
    rows, local = w_query.shape
    heads = width // HEAD_DIM
    scale = HEAD_DIM ** (-0.5)
    head_shape = (images, SEQ, heads, HEAD_DIM)
    attn_shard = jnp.concatenate([w_query, w_key, w_value, w_out], axis=1)
    attn, up, down = (
        full.reshape(n_dp * rows, -1)
        for full in gather_weights((attn_shard, w_up, w_down), n_dp, n_mp)
    )
    both = lax.all_gather(jnp.concatenate([query_bias, value_bias, up_bias]), "mp", axis=0)
    query_bias = both[:, :local].reshape(-1)
    value_bias = both[:, local : 2 * local].reshape(-1)
    up_bias = both[:, 2 * local :].reshape(-1)

    def interleave(*slots):
        return jnp.stack([s.reshape(own_rows, n_mp, local) for s in slots], axis=2).reshape(
            own_rows, -1
        )

    def slot_of(array, slot):
        return array.reshape(own_rows, n_mp, 4, local)[:, :, slot].reshape(own_rows, width)

    inputs = tokens.astype(jnp.float32)
    normed_f, norm1_back = jax.vjp(layer_norm, inputs, ln1_gain, ln1_bias)
    normed = normed_f.astype(jnp.bfloat16)
    projected = matmul(normed, attn)
    queries = (slot_of(projected, 0) + query_bias).astype(jnp.bfloat16).reshape(head_shape)
    keys_low = slot_of(projected, 1).astype(jnp.bfloat16).reshape(head_shape)
    values_low = (slot_of(projected, 2) + value_bias).astype(jnp.bfloat16).reshape(head_shape)
    scaled = (
        jnp.einsum("bqhd,bkhd->bhqk", queries, keys_low, preferred_element_type=jnp.float32) * scale
    )
    row_top = jnp.max(scaled, axis=-1, keepdims=True)
    expos = jnp.exp(scaled - row_top)
    probs = expos / jnp.sum(expos, axis=-1, keepdims=True)
    probs_low = probs.astype(jnp.bfloat16)
    mixed = jnp.einsum("bhqk,bkhd->bqhd", probs_low, values_low, preferred_element_type=jnp.float32)
    mixed = mixed.reshape(own_rows, width).astype(jnp.bfloat16)
    none = jnp.zeros_like(mixed)
    mixed_slots = interleave(none, none, none, mixed)
    middle = inputs + (times_transposed(mixed_slots, attn) + out_bias)
    normed2_f, norm2_back = jax.vjp(layer_norm, middle, ln2_gain, ln2_bias)
    normed2 = normed2_f.astype(jnp.bfloat16)
    upper = matmul(normed2, up) + up_bias
    hidden_f, gelu_back = jax.vjp(gelu_exact, upper)
    hidden = hidden_f.astype(jnp.bfloat16)
    output = middle + (times_transposed(hidden, down) + down_bias)
    activations = output.astype(jnp.bfloat16)
    grad_out = cotangent.astype(jnp.float32)
    grad_branch2 = cotangent
    down_bias_part = column_sums(grad_branch2)
    down_part = contract_rows(grad_branch2, hidden).astype(jnp.bfloat16)
    grad_upper = gelu_back(matmul(grad_branch2, down))[0].astype(jnp.bfloat16)
    up_bias_part = column_sums(grad_upper)
    up_part = contract_rows(normed2, grad_upper).astype(jnp.bfloat16)
    grad_normed2 = times_transposed(grad_upper, up)
    grad_mid_norm, ln2_gain_part, ln2_bias_part = norm2_back(grad_normed2)
    grad_middle = grad_out + grad_mid_norm
    grad_branch = grad_middle.astype(jnp.bfloat16)
    out_bias_part = column_sums(grad_branch)
    grad_mixed = slot_of(matmul(grad_branch, attn), 3).astype(jnp.bfloat16).reshape(head_shape)
    grad_probs = jnp.einsum(
        "bqhd,bkhd->bhqk", grad_mixed, values_low, preferred_element_type=jnp.float32
    )
    grad_values = jnp.einsum(
        "bhqk,bqhd->bkhd", probs_low, grad_mixed, preferred_element_type=jnp.float32
    )
    grad_values = grad_values.astype(jnp.bfloat16).reshape(own_rows, width)
    inner = jnp.sum(probs * grad_probs, axis=-1, keepdims=True)
    grad_scores = (probs * (grad_probs - inner) * scale).astype(jnp.bfloat16)
    grad_queries = jnp.einsum(
        "bhqk,bkhd->bqhd", grad_scores, keys_low, preferred_element_type=jnp.float32
    )
    grad_queries = grad_queries.astype(jnp.bfloat16).reshape(own_rows, width)
    grad_keys = jnp.einsum(
        "bhqk,bqhd->bkhd", grad_scores, queries, preferred_element_type=jnp.float32
    )
    grad_keys = grad_keys.astype(jnp.bfloat16).reshape(own_rows, width)
    query_bias_part = column_sums(grad_queries)
    value_bias_part = column_sums(grad_values)
    grad_slots = interleave(grad_queries, grad_keys, grad_values, none)
    attn_part = contract_rows(
        jnp.concatenate([normed, grad_branch], axis=0),
        jnp.concatenate([grad_slots, mixed_slots], axis=0),
    ).astype(jnp.bfloat16)
    grad_normed = times_transposed(grad_slots, attn)
    grad_in_norm, ln1_gain_part, ln1_bias_part = norm1_back(grad_normed)
    input_grad = grad_middle + grad_in_norm
    vectors = jnp.concatenate(
        [
            ln1_gain_part,
            ln1_bias_part,
            out_bias_part,
            ln2_gain_part,
            ln2_bias_part,
            down_bias_part,
            query_bias_part,
            value_bias_part,
            up_bias_part,
        ]
    ).reshape(-1, width)
    sums, vector_sums = reduce_gradients(
        [part.reshape(n_dp, rows, -1) for part in (down_part, up_part, attn_part)],
        vectors,
        n_dp,
        n_mp,
    )
    at = lax.axis_index("mp")
    up_width = w_up.shape[1]
    own_up = lax.dynamic_slice_in_dim(vector_sums[8:].reshape(-1), at * up_width, up_width)
    return (
        activations,
        input_grad,
        vector_sums[0],
        vector_sums[1],
        sums[2, :, :local],
        lax.dynamic_slice_in_dim(vector_sums[6], at * local, local),
        sums[2, :, local : 2 * local],
        sums[2, :, 2 * local : 3 * local],
        lax.dynamic_slice_in_dim(vector_sums[7], at * local, local),
        sums[2, :, 3 * local :],
        vector_sums[2],
        vector_sums[3],
        vector_sums[4],
        sums[1],
        own_up,
        sums[0],
        vector_sums[5],
    )


def solution(mesh):
    whole, rows, block, ends = P(), P(("dp", "mp"), None), P("dp", "mp"), P("mp")
    in_specs = (
        rows, rows, whole, whole, block, ends, block, block, ends, block,
        whole, whole, whole, block, ends, block, whole,
    )
    out_specs = (
        rows, rows, whole, whole, block, ends, block, block, ends, block,
        whole, whole, whole, block, ends, block, whole,
    )
    return jax.shard_map(
        functools.partial(per_device, mesh.shape["dp"], mesh.shape["mp"]),
        mesh=mesh,
        in_specs=in_specs,
        out_specs=out_specs,
        check_vma=False,
    )
```

time: 571 us -> 318 us (0.56)
  blocking collectives: 281 us -> 13.3 us
  Pallas kernels: 0 us -> 186 us
  waiting for transfers between devices: 147 us -> 0 us
  between operations: 16 us -> 1.65 us
  starting transfers between devices: 8.36 us -> 0 us
    unnamed x3 -> x0, blocking collectives: 191 us -> none
    pallas_call x0 -> x2, Pallas kernels: none -> 186 us  [the longest x1 98.8 us: gather_weights(): pl.pallas_call(functools.partial(gather_kernel, n_dp, n_mp, halves, n_mat...]
    all_gather x6 -> x0, waiting for transfers between devices: 104 us -> none  [the longest x1 30.6 us: per_device(): group_grad1 = lax.all_gather(grad_branch, 'mp', axis=0, tiled=True)]
    psum x2 -> x0, blocking collectives: 52.2 us -> none  [the longest x1 38.7 us: per_device(): lax.psum((ln1_gain_part, ln1_bias_part, out_bias_part, ln2_gain_part, ln2...]
    reduce_scatter x5 -> x0, waiting for transfers between devices: 39.1 us -> none  [the longest x1 39.1 us: per_device(): lax.psum_scatter(w_up_part, 'dp', scatter_dimension=0, tiled=True)]
    all_gather x4 -> x1, blocking collectives: 38.8 us -> 13.3 us  [per_device(): lax.all_gather(jnp.concatenate([query_bias, value_bias, up_bias]), 'mp',...]
    unnamed x90 -> x66, local copies, waits for them, and re-layouts: 22.3 us -> 1.42 us
    another operation x0 -> x2, other arithmetic: none -> 9 us  [interleave(): jnp.stack([s.reshape(own_rows, n_mp, local) for s in slots], axis=2)]
  transfers between devices with their start and end apart: 16 -> 0, of which waited for: 7 -> 0; matrix products, arithmetic and copies ran while one was open for 40% -> 0% of each run, Pallas kernels for 0% -> 0%
where the time goes in v1:
time: 318 us; the launch traced here: 314 us
  Pallas kernels  186 us (58%)
  matrix products  68.1 us (21%)
  local copies, waits for them, and re-layouts  28.9 us (9%)
  other arithmetic  16.5 us (5%)
  blocking collectives  13.3 us (4%)
    pallas_call x1, Pallas kernels, gather_weights(): pl.pallas_call(functools.partial(gather_kernel, n_dp, n_mp, halves, n_mat...  98.8 us
    pallas_call x1, Pallas kernels, reduce_gradients(): pl.pallas_call(functools.partial(reduce_kernel, n_dp, n_mp, halves, n_mat...  86.9 us
    dot_general x4, matrix products, matmul(): return jnp.dot(left, right, preferred_element_type=jnp.float32)  18.7 us
    dot_general x4, matrix products, times_transposed(): lax.dot_general(left, right, (((1,), (1,)), ((), ())), preferred_element_...  18.5 us
    all_gather x1, blocking collectives, per_device(): lax.all_gather(jnp.concatenate([query_bias, value_bias, up_bias]), 'mp',...  13.3 us
    dot_general x3, matrix products, contract_rows(): lax.dot_general(left, right, (((0,), (0,)), ((), ())), preferred_element_...  11.4 us
    another operation x2, other arithmetic, interleave(): jnp.stack([s.reshape(own_rows, n_mp, local) for s in slots], axis=2)  9 us
    another operation x5, local copies, waits for them, and re-layouts, interleave(): jnp.stack([s.reshape(own_rows, n_mp, local) for s in slots], axis=2)  7.53 us

profile of v1, /device:TPU:0, one launch (start us, length us, event | category | flops | bytes accessed | tf_op | source)
XLA Modules:
  0.0 314.2 jit_solution(8145111862807029371)
XLA Ops:
  5.9 98.8 %shard_map.296 = (bf16[8,96,3072]{2,1,0:T(8,128)(2,1)}, bf16[8,96,3072]{2,1,0:T(8,128)(2,1)}, bf16[8,96,3072]{2,1,0:T(8,128)(2,1)}) custom-call(bf16[96,768]{1,0:T(8,128)(2,1)} %pad_maximum_fusion.2.refs_0_, bf16[96,768]{1,0:T(8,128)(2,1)} %refs_1_.1, bf16[96,768]{1,0:T(8,128)(2,1)} %refs_2_.1), custom_call_target="tpu_custom_call" | custom-call | tf_op jit(solution)/shard_map/pallas_call | solution.py:181
  104.7 6.7 %copy.50 = bf16[3072,768]{1,0:T(8,128)(2,1)} copy(bf16[3072,768]{0,1:T(8,128)(2,1)} %bitcast.95) | data formatting | bytes 9437184 | tf_op jit(solution)/shard_map/dot_general | solution.py:29
  111.4 3.7 %fusion.54 = f32[197,4,4,192]{0,3,2,1:T(8,128)S(1)} fusion(bf16[4,4,192,768]{3,2,1,0:T(8,128)(2,1)} %bitcast.91, bf16[197,768]{1,0:T(8,128)(2,1)S(1)} %fusion.42), kind=kOutput, calls=%fused_computation.88 | convolution fusion | flops 929562624 | bytes 7441920 | tf_op jit(solution)/shard_map/dot_general | solution.py:29
  116.0 13.3 %all-gather.1 = f32[4,1,1152]{2,1,0:T(1,128)S(1)} all-gather(f32[1,1,1152]{2,1,0:T(1,128)S(1)} %reshape.257), channel_id=2, replica_groups=mesh['dp'=8,'mp'=4] {'mp'}, dimensions={0}, use_global_device_ids=true | all-gather | bytes 23040 | tf_op jit(solution)/shard_map/all_gather | solution.py:453
  129.4 2.5 fusion.75
  132.0 2.1 convolution_convert_fusion.4
  136.7 3.3 %pad_maximum_fusion = bf16[197,4,4,192]{3,2,1,0:T(4,128)(2,1)S(1)} fusion(bf16[197,4,1,192]{3,2,1,0:T(2,128)(2,1)} %copy.52, bf16[197,4,1,192]{3,2,1,0:T(2,128)(2,1)S(1)} %broadcast.116, bf16[4]{0:T(256)(128)(2,1)S(1)} %pad.9.clone), kind=kLoop, calls=%fused_computation.36 | loop fusion | flops 3631104 | bytes 1815560 | tf_op jit(solution)/shard_map/stack | solution.py:459
  140.0 3.3 %reshape.247 = bf16[197,3072]{1,0:T(8,128)(2,1)} reshape(bf16[197,4,4,192]{3,2,1,0:T(4,128)(2,1)S(1)} %pad_maximum_fusion) | data formatting | bytes 2420736 | tf_op jit(solution)/shard_map/reshape | solution.py:459
  143.3 4.5 %fusion.76 = (f32[197]{0:T(256)S(1)}, f32[197,768]{1,0:T(8,128)S(1)}) fusion(f32[768]{0:T(1024)S(1)} %copy-done.24, bf16[197,3072]{1,0:T(8,128)(2,1)} %reshape.247, bf16[768,3072]{1,0:T(8,128)(2,1)} %bitcast.96, bf16[197,768]{1,0:T(8,128)(2,1)S(1)} %copy-done), kind=kOutput, calls=%fused_computation.140 | convolution fusion | flops 930167616 | bytes 6840596 | tf_op jit(solution)/shard_map/dot_general | solution.py:39
  148.0 9.0 %multiply_convert_fusion.1 = (bf16[197,3072]{1,0:T(8,128)(2,1)}, f32[197,3072]{1,0:T(8,128)S(1)}, f32[197,3072]{1,0:T(8,128)S(1)}) fusion(f32[3072]{0:T(1024)S(1)} %add.122, bf16[768,3072]{1,0:T(8,128)(2,1)} %bitcast.117, f32[197,768]{1,0:T(8,128)S(1)} %get-tuple-element.69, f32[768]{0:T(1024)S(1)} %copy-done.19, f32[768]{0:T(1024)S(1)} %copy-done.18, ...), kind=kOutput, calls=%fused_computation.17 | convolution fusion | flops 970261248 | bytes 11395624 | tf_op jit(solution)/shard_map/dot_general | solution.py:29
  157.0 4.5 %convert_reduce_fusion = (f32[3072]{0:T(1024)S(1)}, bf16[197,3072]{1,0:T(8,128)(2,1)S(1)}) fusion(f32[197,3072]{1,0:T(8,128)S(1)} %get-tuple-element.45, f32[197,3072]{1,0:T(8,128)S(1)} %get-tuple-element.70, bf16[768,3072]{1,0:T(8,128)(2,1)} %bitcast.115, bf16[197,768]{1,0:T(8,128)(2,1)S(1)} %copy-done.8), kind=kOutput, calls=%fused_computation.12 | convolution fusion | flops 939242496 | bytes 11085312 | tf_op jit(solution)/shard_map/dot_general | solution.py:29
  161.5 4.7 %multiply_reduce_fusion.2 = (f32[768]{0:T(1024)S(1)}, f32[197]{0:T(256)S(1)}, f32[768]{0:T(1024)S(1)}, f32[197,768]{1,0:T(8,128)S(1)}) fusion(f32[197,768]{1,0:T(8,128)S(1)} %get-tuple-element.69, f32[197]{0:T(256)S(1)} %fusion.60, f32[197]{0:T(256)S(1)} %broadcast_multiply_fusion, f32[768]{0:T(1024)S(1)} %copy-done.18, ...), kind=kOutput, calls=%fused_computation.77 | convolution fusion | flops 930771264 | bytes 7150908 | tf_op jit(solution)/shard_map/dot_general | solution.py:39
  169.2 2.3 fusion.58
  171.4 5.6 %convert_reduce_fusion.3 = (f32[12,64]{1,0:T(8,128)S(1)}, bf16[12,64,197]{2,1,0:T(8,128)(2,1)}) fusion(bf16[197,12,64]{0,2,1:T(8,128)(2,1)S(1)} %bitcast.104, f32[12,197,197]{1,2,0:T(8,128)} %fusion.58, f32[12,197,197]{1,2,0:T(8,128)} %get-tuple-element.67, f32[12,197]{1,0:T(8,128)S(1)} %get-tuple-element.66), kind=kOutput, calls=%fused_computation.62 | convolution fusion | flops 63326260 | bytes 4343376 | tf_op jit(solution)/shard_map/bhqk,bkhd->bqhd/dot_general | solution.py:514
  177.1 3.5 %copy.56 = bf16[197,4,1,192]{3,2,1,0:T(2,128)(2,1)} copy(bf16[197,4,1,192]{0,3,1,2:T(8,128)(2,1)} %bitcast.108) | data formatting | bytes 605184 | tf_op jit(solution)/shard_map/stack;reshape;reshape | solution.py:459
  180.6 4.8 %fusion.26 = bf16[12,64,197]{2,1,0:T(8,128)(2,1)S(1)} fusion(f32[12,197,197]{1,2,0:T(8,128)} %fusion.58, f32[12,197,197]{1,2,0:T(8,128)} %get-tuple-element.67, f32[12,197]{1,0:T(8,128)S(1)} %get-tuple-element.66, f32[197,12,64]{0,2,1:T(8,128)S(1)} %bitcast.100, f32[12,64]{1,0:T(8,128)S(1)} %add.113), kind=kOutput, calls=%fused_computation.39 | convolution fusion | flops 63327028 | bytes 4645968 | tf_op jit(solution)/shard_map/bhqk,bqhd->bkhd/dot_general | solution.py:518
  187.3 2.3 convert_reduce_fusion.2
  191.6 5.7 %pad_maximum_fusion.1 = bf16[197,4,4,192]{3,2,1,0:T(4,128)(2,1)S(1)} fusion(bf16[197,4,1,192]{3,2,1,0:T(2,128)(2,1)S(1)} %broadcast.116, bf16[197,4,1,192]{3,2,1,0:T(2,128)(2,1)} %copy.58, bf16[197,4,1,192]{3,2,1,0:T(2,128)(2,1)} %copy.57, bf16[197,4,1,192]{3,2,1,0:T(2,128)(2,1)} %copy.56), kind=kLoop, calls=%fused_computation.37 | loop fusion | flops 4841472 | bytes 2420736 | tf_op jit(solution)/shard_map/stack | solution.py:459
  197.3 3.3 %reshape.250 = bf16[197,3072]{1,0:T(8,128)(2,1)} reshape(bf16[197,4,4,192]{3,2,1,0:T(4,128)(2,1)S(1)} %pad_maximum_fusion.1) | data formatting | bytes 2420736 | tf_op jit(solution)/shard_map/reshape | solution.py:459
  200.6 4.5 %fusion.68 = (f32[768]{0:T(1024)S(1)}, f32[197]{0:T(256)S(1)}, f32[197,768]{1,0:T(8,128)S(1)}) fusion(f32[768]{0:T(1024)S(1)} %copy-done.20, f32[197]{0:T(256)S(1)} %broadcast_multiply_fusion.1, bf16[197,768]{1,0:T(8,128)(2,1)S(1)} %copy-done, bf16[197,3072]{1,0:T(8,128)(2,1)} %reshape.250, bf16[768,3072]{1,0:T(8,128)(2,1)} %bitcast.97), kind=kOutput, calls=%fused_computation.134 | convolution fusion | flops 930469440 | bytes 6844456 | tf_op jit(solution)/shard_map/dot_general | solution.py:39
  207.0 6.2 %convolution_convert_fusion.2 = bf16[768,3072]{1,0:T(8,128)(2,1)} fusion(bf16[197,3072]{1,0:T(8,128)(2,1)} %reshape.247, bf16[197,3072]{1,0:T(8,128)(2,1)} %reshape.250, bf16[197,768]{1,0:T(8,128)(2,1)S(1)} %copy-done.17, bf16[197,768]{1,0:T(8,128)(2,1)S(1)} %copy-done.13), kind=kOutput, calls=%fused_computation.4 | convolution fusion | flops 1867536384 | bytes 7744512 | tf_op jit(solution)/shard_map/dot_general | solution.py:33
  213.2 3.8 %convolution_convert_fusion = bf16[768,3072]{1,0:T(8,128)(2,1)} fusion(bf16[197,3072]{1,0:T(8,128)(2,1)S(1)} %copy-done.15, f32[197,768]{1,0:T(8,128)S(1)} %get-tuple-element.69, f32[768]{0:T(1024)S(1)} %copy-done.19, f32[768]{0:T(1024)S(1)} %copy-done.18, f32[197]{0:T(256)S(1)} %fusion.60, f32[197]{0:T(256)S(1)} %broadcast_multiply_fusion), kind=kOutput, calls=%fused_computation.2 | convolution fusion | flops 932678400 | bytes 6541864 | tf_op jit(solution)/shard_map/dot_general | solution.py:33
  218.5 86.9 %shard_map.297 = (f32[3,96,768]{2,1,0:T(8,128)S(1)}, f32[12,768]{1,0:T(8,128)S(1)}) custom-call(bf16[8,96,3072]{2,1,0:T(8,128)(2,1)S(1)} %bitcast.89, bf16[8,96,3072]{2,1,0:T(8,128)(2,1)} %bitcast.90, bf16[8,96,3072]{2,1,0:T(8,128)(2,1)} %bitcast.98, f32[12,768]{1,0:T(8,128)S(1)} %reshape.254.refs_3_), custom_call_target="tpu_custom_call" | custom-call | tf_op jit(solution)/shard_map/pallas_call | solution.py:395
  309.0 4.8 %fusion.34 = bf16[197,768]{1,0:T(8,128)(2,1)} fusion(f32[197,768]{1,0:T(8,128)S(1)} %get-tuple-element.69, bf16[197,3072]{1,0:T(8,128)(2,1)S(1)} %copy-done.7, bf16[768,3072]{1,0:T(8,128)(2,1)} %bitcast.116, f32[768]{0:T(1024)S(1)} %copy-done.25), kind=kOutput, calls=%fused_computation.50 | convolution fusion | flops 930016512 | bytes 6839808 | tf_op jit(solution)/shard_map/dot_general | solution.py:39
  (113 shorter events, 22.6 us)
Async XLA Ops:
  4.2 107.2 %copy-start.12 = (bf16[197,768]{1,0:T(8,128)(2,1)}, bf16[197,768]{1,0:T(8,128)(2,1)S(1)}, u32[]{:S(2)}) copy-start(bf16[197,768]{1,0:T(8,128)(2,1)S(1)} %fusion.42) | copy-start | bytes 907780
  115.4 18.7 %copy-start.3 = (f32[197,4,1,192]{0,3,2,1:T(8,128)}, f32[197,4,1,192]{0,3,2,1:T(8,128)S(1)}, u32[]{:S(2)}) copy-start(f32[197,4,1,192]{0,3,2,1:T(8,128)S(1)} %get-tuple-element.46) | copy-start | bytes 1815556
  115.4 18.7 %copy-start.5 = (f32[197,4,1,192]{0,3,2,1:T(8,128)}, f32[197,4,1,192]{0,3,2,1:T(8,128)S(1)}, u32[]{:S(2)}) copy-start(f32[197,4,1,192]{0,3,2,1:T(8,128)S(1)} %get-tuple-element.47) | copy-start | bytes 1815556
  115.5 18.7 %copy-start.10 = (bf16[197,4,1,192]{0,3,2,1:T(8,128)(2,1)}, bf16[197,4,1,192]{0,3,2,1:T(8,128)(2,1)S(1)}, u32[]{:S(2)}) copy-start(bf16[197,4,1,192]{0,3,2,1:T(8,128)(2,1)S(1)} %slice.112) | copy-start | bytes 907780
  136.6 6.6 %copy-start = (bf16[197,768]{1,0:T(8,128)(2,1)S(1)}, bf16[197,768]{1,0:T(8,128)(2,1)}, u32[]{:S(2)}) copy-start(bf16[197,768]{1,0:T(8,128)(2,1)} %param.17) | copy-start | bytes 907780
  136.7 6.6 %copy-start.24 = (f32[768]{0:T(1024)S(1)}, f32[768]{0:T(1024)}, u32[]{:S(2)}) copy-start(f32[768]{0:T(1024)} %param.27) | copy-start | bytes 9220
  143.3 4.7 %copy-start.18 = (f32[768]{0:T(1024)S(1)}, f32[768]{0:T(1024)}, u32[]{:S(2)}) copy-start(f32[768]{0:T(1024)} %param.28) | copy-start | bytes 9220
  143.3 4.8 %copy-start.19 = (f32[768]{0:T(1024)S(1)}, f32[768]{0:T(1024)}, u32[]{:S(2)}) copy-start(f32[768]{0:T(1024)} %param.29) | copy-start | bytes 9220
  148.0 9.0 %copy-start.8 = (bf16[197,768]{1,0:T(8,128)(2,1)S(1)}, bf16[197,768]{1,0:T(8,128)(2,1)}, u32[]{:S(2)}) copy-start(bf16[197,768]{1,0:T(8,128)(2,1)} %param.18) | copy-start | bytes 907780
  161.5 4.7 %copy-start.14 = (bf16[197,3072]{1,0:T(8,128)(2,1)}, bf16[197,3072]{1,0:T(8,128)(2,1)S(1)}, u32[]{:S(2)}) copy-start(bf16[197,3072]{1,0:T(8,128)(2,1)S(1)} %get-tuple-element.78) | copy-start | bytes 3631108
  161.5 6.1 %slice-start = ((s8[4718592]{0:T(1024)(128)(4,1)}), s8[4194304]{0:T(1024)(128)(4,1)S(1)}, s32[]{:S(2)}) async-start(s8[4718592]{0:T(1024)(128)(4,1)} %bitcast.92), calls=%async_computation | async-start | bytes 8388608
  161.5 6.1 %slice-start.1 = ((s8[4718592]{0:T(1024)(128)(4,1)}), s8[524288]{0:T(1024)(128)(4,1)S(1)}, s32[]{:S(2)}) async-start(s8[4718592]{0:T(1024)(128)(4,1)} %bitcast.92), calls=%async_computation.1 | async-start | bytes 1048576
  167.6 1.5 copy-start.16
  167.6 1.6 copy-start.6
  169.1 2.3 copy-start.11
  171.4 9.2 %copy-start.4 = (f32[197,4,1,192]{0,3,2,1:T(8,128)S(1)}, f32[197,4,1,192]{0,3,2,1:T(8,128)}, u32[]{:S(2)}) copy-start(f32[197,4,1,192]{0,3,2,1:T(8,128)} %copy-done.3) | copy-start | bytes 1815556
  197.3 3.3 %copy-start.20 = (f32[768]{0:T(1024)S(1)}, f32[768]{0:T(1024)}, u32[]{:S(2)}) copy-start(f32[768]{0:T(1024)} %param.19) | copy-start | bytes 9220
  200.6 5.1 %copy-start.2 = (f32[197,768]{1,0:T(8,128)S(1)}, f32[197,768]{1,0:T(8,128)}, u32[]{:S(2)}) copy-start(f32[197,768]{1,0:T(8,128)} %copy-done.1) | copy-start | bytes 1815556
  200.6 5.1 %copy-start.9 = (bf16[197,768]{1,0:T(8,128)(2,1)S(1)}, bf16[197,768]{1,0:T(8,128)(2,1)}, u32[]{:S(2)}) copy-start(bf16[197,768]{1,0:T(8,128)(2,1)} %param.18) | copy-start | bytes 907780
  205.1 1.9 copy-start.13
  205.1 1.9 copy-start.17
  207.0 6.2 %copy-start.15 = (bf16[197,3072]{1,0:T(8,128)(2,1)S(1)}, bf16[197,3072]{1,0:T(8,128)(2,1)}, u32[]{:S(2)}) copy-start(bf16[197,3072]{1,0:T(8,128)(2,1)} %copy-done.14) | copy-start | bytes 3631108
  213.2 3.8 %copy-start.7 = (bf16[197,3072]{1,0:T(8,128)(2,1)S(1)}, bf16[197,3072]{1,0:T(8,128)(2,1)}, u32[]{:S(2)}) copy-start(bf16[197,3072]{1,0:T(8,128)(2,1)} %get-tuple-element.44) | copy-start | bytes 3631108
  218.5 90.6 %copy-start.25 = (f32[768]{0:T(1024)S(1)}, f32[768]{0:T(1024)}, u32[]{:S(2)}) copy-start(f32[768]{0:T(1024)} %param.33) | copy-start | bytes 9220
  (4 other events, 2.9 us)

commit v2 on v1

--- a/solution.py
+++ b/solution.py
@@ -94,8 +94,9 @@
 
 
 def gather_kernel(n_dp, n_mp, halves, n_mats, *refs):
-    shards, outs = refs[:n_mats], refs[n_mats : 2 * n_mats]
-    send_sem, recv_sem, own_sem = refs[2 * n_mats :]
+    shards, bias = refs[:n_mats], refs[n_mats]
+    outs, bias_all = refs[n_mats + 1 : 2 * n_mats + 1], refs[2 * n_mats + 1]
+    send_sem, recv_sem, own_sem, bias_send, bias_recv = refs[2 * n_mats + 2 :]
     dp_bits, mp_bits = bits_in(n_dp), bits_in(n_mp)
     rows, width = shards[0].shape
     piece = rows // halves
@@ -124,6 +125,31 @@
     sent = []
     waiting = {}
     n_stages = dp_bits + mp_bits
+    bias_all[mp] = bias[...]
+    bias_wait = []
+
+    def bias_run(stage):
+        _, bit, _, done_mp = gather_plan(dp_bits, mp_bits, 0)[stage]
+        slot = (1 << stage) - 1
+        for number, (m, their_m) in enumerate(
+            zip(subsets(mp, done_mp), subsets(flip(mp, bit), done_mp))
+        ):
+            sems = dict(
+                send_sem=bias_send.at[slot + number],
+                recv_sem=bias_recv.at[slot + number],
+                device_id=(dp, flip(mp, bit)),
+                device_id_type=MESH,
+            )
+            copy = pltpu.make_async_remote_copy(
+                src_ref=bias_all.at[m], dst_ref=bias_all.at[m], **sems
+            )
+            copy.start()
+            sent.append(copy)
+            bias_wait.append(
+                pltpu.make_async_remote_copy(
+                    src_ref=bias_all.at[their_m], dst_ref=bias_all.at[their_m], **sems
+                )
+            )
 
     def run(mat, half, stage):
         variant = half if halves > 1 else mat % 2
@@ -162,6 +188,11 @@
             copy.wait_recv()
 
     for step in range(n_mats + n_stages):
+        if step <= mp_bits:
+            while bias_wait:
+                bias_wait.pop().wait_recv()
+            if step < mp_bits:
+                bias_run(step)
         for stage in range(n_stages + 1)[::-1]:
             mat = step - stage
             if 0 <= mat < n_mats:
@@ -173,23 +204,28 @@
         copy.wait_send()
 
 
-def gather_weights(shards, n_dp, n_mp):
+def gather_weights(shards, bias, n_dp, n_mp):
     rows, width = shards[0].shape
     n_mats = len(shards)
     halves = 2 if rows % 32 == 0 else 1
     copies = (n_mp - 1) + (n_dp - 1)
     return pl.pallas_call(
         functools.partial(gather_kernel, n_dp, n_mp, halves, n_mats),
-        out_shape=[jax.ShapeDtypeStruct((n_dp, rows, n_mp * width), jnp.bfloat16)] * n_mats,
-        in_specs=[pl.BlockSpec(memory_space=pl.ANY)] * n_mats,
-        out_specs=[pl.BlockSpec(memory_space=pl.ANY)] * n_mats,
+        out_shape=[jax.ShapeDtypeStruct((n_dp, rows, n_mp * width), jnp.bfloat16)] * n_mats
+        + [jax.ShapeDtypeStruct((n_mp,) + bias.shape, jnp.float32)],
+        in_specs=[pl.BlockSpec(memory_space=pl.ANY)] * n_mats
+        + [pl.BlockSpec(memory_space=pltpu.VMEM)],
+        out_specs=[pl.BlockSpec(memory_space=pl.ANY)] * n_mats
+        + [pl.BlockSpec(memory_space=pltpu.VMEM)],
         scratch_shapes=[
             pltpu.SemaphoreType.DMA((n_mats * halves, copies)),
             pltpu.SemaphoreType.DMA((n_mats * halves, copies)),
             pltpu.SemaphoreType.DMA((n_mats,)),
+            pltpu.SemaphoreType.DMA((max(n_mp - 1, 1),)),
+            pltpu.SemaphoreType.DMA((max(n_mp - 1, 1),)),
         ],
         compiler_params=pltpu.CompilerParams(collective_id=0, has_side_effects=True),
-    )(*shards)
+    )(*shards, bias)
 
 
 def reduce_kernel(n_dp, n_mp, halves, n_mats, *refs):
@@ -446,19 +482,21 @@
     scale = HEAD_DIM ** (-0.5)
     head_shape = (images, SEQ, heads, HEAD_DIM)
     attn_shard = jnp.concatenate([w_query, w_key, w_value, w_out], axis=1)
-    attn, up, down = (
-        full.reshape(n_dp * rows, -1)
-        for full in gather_weights((attn_shard, w_up, w_down), n_dp, n_mp)
-    )
-    both = lax.all_gather(jnp.concatenate([query_bias, value_bias, up_bias]), "mp", axis=0)
+    bias = jnp.concatenate([query_bias, value_bias, up_bias])
+    *weights, both = gather_weights((attn_shard, w_up, w_down), bias.reshape(-1, 128), n_dp, n_mp)
+    attn, up, down = (full.reshape(n_dp * rows, -1) for full in weights)
+    both = both.reshape(n_mp, -1)
     query_bias = both[:, :local].reshape(-1)
     value_bias = both[:, local : 2 * local].reshape(-1)
     up_bias = both[:, 2 * local :].reshape(-1)
 
+    near = local // HEAD_DIM
+
     def interleave(*slots):
-        return jnp.stack([s.reshape(own_rows, n_mp, local) for s in slots], axis=2).reshape(
-            own_rows, -1
+        stacked = jnp.stack(
+            [s.reshape(images, n_mp, near, SEQ, HEAD_DIM) for s in slots], axis=2
         )
+        return stacked.transpose(0, 4, 1, 2, 3, 5).reshape(own_rows, -1)
 
     def slot_of(array, slot):
         return array.reshape(own_rows, n_mp, 4, local)[:, :, slot].reshape(own_rows, width)
@@ -477,8 +515,8 @@
     expos = jnp.exp(scaled - row_top)
     probs = expos / jnp.sum(expos, axis=-1, keepdims=True)
     probs_low = probs.astype(jnp.bfloat16)
-    mixed = jnp.einsum("bhqk,bkhd->bqhd", probs_low, values_low, preferred_element_type=jnp.float32)
-    mixed = mixed.reshape(own_rows, width).astype(jnp.bfloat16)
+    mixed = jnp.einsum("bhqk,bkhd->bhqd", probs_low, values_low, preferred_element_type=jnp.float32)
+    mixed = mixed.astype(jnp.bfloat16)
     none = jnp.zeros_like(mixed)
     mixed_slots = interleave(none, none, none, mixed)
     middle = inputs + (times_transposed(mixed_slots, attn) + out_bias)
@@ -506,21 +544,21 @@
         "bqhd,bkhd->bhqk", grad_mixed, values_low, preferred_element_type=jnp.float32
     )
     grad_values = jnp.einsum(
-        "bhqk,bqhd->bkhd", probs_low, grad_mixed, preferred_element_type=jnp.float32
-    )
-    grad_values = grad_values.astype(jnp.bfloat16).reshape(own_rows, width)
+        "bhqk,bqhd->bhkd", probs_low, grad_mixed, preferred_element_type=jnp.float32
+    )
+    grad_values = grad_values.astype(jnp.bfloat16)
     inner = jnp.sum(probs * grad_probs, axis=-1, keepdims=True)
     grad_scores = (probs * (grad_probs - inner) * scale).astype(jnp.bfloat16)
     grad_queries = jnp.einsum(
-        "bhqk,bkhd->bqhd", grad_scores, keys_low, preferred_element_type=jnp.float32
-    )
-    grad_queries = grad_queries.astype(jnp.bfloat16).reshape(own_rows, width)
+        "bhqk,bkhd->bhqd", grad_scores, keys_low, preferred_element_type=jnp.float32
+    )
+    grad_queries = grad_queries.astype(jnp.bfloat16)
     grad_keys = jnp.einsum(
-        "bhqk,bqhd->bkhd", grad_scores, queries, preferred_element_type=jnp.float32
-    )
-    grad_keys = grad_keys.astype(jnp.bfloat16).reshape(own_rows, width)
-    query_bias_part = column_sums(grad_queries)
-    value_bias_part = column_sums(grad_values)
+        "bhqk,bqhd->bhkd", grad_scores, queries, preferred_element_type=jnp.float32
+    )
+    grad_keys = grad_keys.astype(jnp.bfloat16)
+    query_bias_part = jnp.sum(grad_queries.astype(jnp.float32), axis=(0, 2)).reshape(-1)
+    value_bias_part = jnp.sum(grad_values.astype(jnp.float32), axis=(0, 2)).reshape(-1)
     grad_slots = interleave(grad_queries, grad_keys, grad_values, none)
     attn_part = contract_rows(
         jnp.concatenate([normed, grad_branch], axis=0),

time: 318 us -> 279 us (0.88)
  local copies, waits for them, and re-layouts: 28.9 us -> 14.8 us
  blocking collectives: 13.3 us -> 0 us
  other arithmetic: 16.5 us -> 9.38 us
    all_gather x1 -> x0, blocking collectives: 13.3 us -> none  [per_device(): lax.all_gather(jnp.concatenate([query_bias, value_bias, up_bias]), 'mp',...]
    another operation x2, other arithmetic: 9 us -> 0.56 us  [interleave(): jnp.stack([s.reshape(images, n_mp, near, SEQ, HEAD_DIM) for s in slots],...]
    another operation x6 -> x3, local copies, waits for them, and re-layouts: 7.95 us -> 0.11 us  [the longest x2 0.08 us: interleave(): jnp.stack([s.reshape(images, n_mp, near, SEQ, HEAD_DIM) for s in slots],...]
    reshape x2, local copies, waits for them, and re-layouts: 6.55 us -> 0.14 us  [the longest x1 0.07 us: per_device(): jnp.sum(grad_queries.astype(jnp.float32), axis=(0, 2)).reshape(-1)]
    pallas_call x1, Pallas kernels: 86.9 us -> 82.1 us  [reduce_gradients(): pl.pallas_call(functools.partial(reduce_kernel, n_dp, n_mp, halves, n_mat...]
where the time goes in v2:
time: 279 us; the launch traced here: 278 us
  Pallas kernels  183 us (66%)
  matrix products  69.1 us (25%)
  local copies, waits for them, and re-layouts  14.8 us (5%)
  other arithmetic  9.38 us (3%)
    pallas_call x1, Pallas kernels, gather_weights(): pl.pallas_call(functools.partial(gather_kernel, n_dp, n_mp, halves, n_mat...  101 us
    pallas_call x1, Pallas kernels, reduce_gradients(): pl.pallas_call(functools.partial(reduce_kernel, n_dp, n_mp, halves, n_mat...  82.1 us
    dot_general x4, matrix products, matmul(): return jnp.dot(left, right, preferred_element_type=jnp.float32)  19 us
    dot_general x4, matrix products, times_transposed(): lax.dot_general(left, right, (((1,), (1,)), ((), ())), preferred_element_...  16 us
    dot_general x3, matrix products, contract_rows(): lax.dot_general(left, right, (((0,), (0,)), ((), ())), preferred_element_...  13.2 us
    dot_general x1, local copies, waits for them, and re-layouts, matmul(): return jnp.dot(left, right, preferred_element_type=jnp.float32)  6.71 us

profile of v2, /device:TPU:0, one launch (start us, length us, event | category | flops | bytes accessed | tf_op | source)
XLA Modules:
  0.0 277.9 jit_solution(8275678706023451026)
XLA Ops:
  1.8 1.2 fusion.44
  3.0 1.2 fusion.42
  4.2 1.8 pad_maximum_fusion.2.refs_0_
  6.0 1.4 concatenate.16
  7.3 101.1 %shard_map.296 = (bf16[8,96,3072]{2,1,0:T(8,128)(2,1)}, bf16[8,96,3072]{2,1,0:T(8,128)(2,1)}, bf16[8,96,3072]{2,1,0:T(8,128)(2,1)}, f32[4,9,128]{2,1,0:T(8,128)}) custom-call(bf16[96,768]{1,0:T(8,128)(2,1)} %pad_maximum_fusion.2.refs_0_, bf16[96,768]{1,0:T(8,128)(2,1)} %refs_1_.1, bf16[96,768]{1,0:T(8,128)(2,1)} %refs_2_.1, f32[9,128]{1,0:T(8,128)} %bitcast.117), custom_call_target="tpu_custom_call" | custom-call | tf_op jit(solution)/shard_map/pallas_call | solution.py:212
  108.5 6.7 %copy.41 = bf16[3072,768]{1,0:T(8,128)(2,1)} copy(bf16[3072,768]{0,1:T(8,128)(2,1)} %bitcast.93) | data formatting | bytes 9437184 | tf_op jit(solution)/shard_map/dot_general | solution.py:29
  115.2 3.7 %fusion.54 = f32[197,4,4,192]{0,3,2,1:T(8,128)S(1)} fusion(bf16[4,4,192,768]{3,2,1,0:T(8,128)(2,1)} %bitcast.89, bf16[197,768]{1,0:T(8,128)(2,1)S(1)} %fusion.42), kind=kOutput, calls=%fused_computation.88 | convolution fusion | flops 929562624 | bytes 7441920 | tf_op jit(solution)/shard_map/dot_general | solution.py:29
  119.9 2.5 fusion.75
  122.4 2.1 convolution_convert_fusion.4
  125.5 4.2 %fusion.76 = (f32[197]{0:T(256)S(1)}, f32[197,768]{1,0:T(8,128)S(1)}) fusion(f32[768]{0:T(1024)S(1)} %copy-done.32, bf16[197,3072]{0,1:T(8,128)(2,1)S(1)} %bitcast.103, bf16[768,3072]{1,0:T(8,128)(2,1)} %bitcast.94, bf16[197,768]{1,0:T(8,128)(2,1)S(1)} %copy-done), kind=kOutput, calls=%fused_computation.140 | convolution fusion | flops 930167616 | bytes 6840596 | tf_op jit(solution)/shard_map/dot_general | solution.py:39
  130.0 8.7 %multiply_convert_fusion.1 = (bf16[197,3072]{1,0:T(8,128)(2,1)}, f32[197,3072]{1,0:T(8,128)S(1)}, f32[197,3072]{1,0:T(8,128)S(1)}) fusion(f32[3072]{0:T(1024)S(1)} %add.122, bf16[768,3072]{1,0:T(8,128)(2,1)} %bitcast.123, f32[197,768]{1,0:T(8,128)S(1)} %get-tuple-element.71, f32[768]{0:T(1024)S(1)} %copy-done.17, f32[768]{0:T(1024)S(1)} %copy-done.16, ...), kind=kOutput, calls=%fused_computation.17 | convolution fusion | flops 970261248 | bytes 11395624 | tf_op jit(solution)/shard_map/dot_general | solution.py:29
  138.7 5.1 %convert_reduce_fusion = (f32[3072]{0:T(1024)}, bf16[197,3072]{1,0:T(8,128)(2,1)S(1)}) fusion(f32[197,3072]{1,0:T(8,128)S(1)} %get-tuple-element.47, f32[197,3072]{1,0:T(8,128)S(1)} %get-tuple-element.72, bf16[768,3072]{1,0:T(8,128)(2,1)} %bitcast.121, bf16[197,768]{1,0:T(8,128)(2,1)S(1)} %copy-done.2), kind=kOutput, calls=%fused_computation.12 | convolution fusion | flops 939242496 | bytes 11085312 | tf_op jit(solution)/shard_map/dot_general | solution.py:29
  143.8 5.3 %multiply_reduce_fusion.2 = (f32[768]{0:T(1024)}, f32[197]{0:T(256)S(1)}, f32[768]{0:T(1024)}, f32[197,768]{1,0:T(8,128)S(1)}) fusion(f32[197,768]{1,0:T(8,128)S(1)} %get-tuple-element.71, f32[197]{0:T(256)S(1)} %fusion.60, f32[197]{0:T(256)S(1)} %broadcast_multiply_fusion, f32[768]{0:T(1024)S(1)} %copy-done.16, ...), kind=kOutput, calls=%fused_computation.77 | convolution fusion | flops 930771264 | bytes 7150908 | tf_op jit(solution)/shard_map/dot_general | solution.py:39
  150.9 1.5 fusion.52
  153.1 2.3 fusion.58
  155.4 5.5 %convert_reduce_fusion.3 = (f32[12,64]{1,0:T(8,128)}, bf16[12,197,64]{1,2,0:T(8,128)(2,1)S(1)}) fusion(bf16[197,12,64]{0,2,1:T(8,128)(2,1)} %bitcast.108, f32[12,197,197]{1,2,0:T(8,128)} %fusion.58, f32[12,197,197]{1,2,0:T(8,128)} %get-tuple-element.69, f32[12,197]{1,0:T(8,128)S(1)} %get-tuple-element.68), kind=kOutput, calls=%fused_computation.62 | convolution fusion | flops 63326260 | bytes 4343376 | tf_op jit(solution)/shard_map/bhqk,bkhd->bhqd/dot_general | solution.py:552
  160.9 5.6 %fusion.26 = bf16[12,197,64]{1,2,0:T(8,128)(2,1)} fusion(f32[12,197,197]{1,2,0:T(8,128)} %fusion.58, f32[12,197,197]{1,2,0:T(8,128)} %get-tuple-element.69, f32[12,197]{1,0:T(8,128)S(1)} %get-tuple-element.68, f32[197,12,64]{0,2,1:T(8,128)S(1)} %bitcast.100, f32[12,64]{1,0:T(8,128)S(1)} %add.110), kind=kOutput, calls=%fused_computation.39 | convolution fusion | flops 63327028 | bytes 4645968 | tf_op jit(solution)/shard_map/bhqk,bqhd->bhkd/dot_general | solution.py:556
  166.5 3.1 %convert_reduce_fusion.2 = (f32[12,64]{1,0:T(8,128)}, bf16[12,197,64]{1,2,0:T(8,128)(2,1)S(1)}) fusion(bf16[197,12,64]{0,2,1:T(8,128)(2,1)S(1)} %bitcast.110, f32[12,197,197]{1,2,0:T(8,128)} %get-tuple-element.69, f32[12,197]{1,0:T(8,128)S(1)} %get-tuple-element.68), kind=kOutput, calls=%fused_computation.61 | convolution fusion | flops 60995160 | bytes 2480544 | tf_op jit(solution)/shard_map/bhqk,bqhd->bhkd/dot_general | solution.py:546
  170.3 1.8 fusion.68
  174.1 7.9 %convolution_convert_fusion.2 = bf16[768,3072]{1,0:T(8,128)(2,1)} fusion(bf16[197,3072]{0,1:T(8,128)(2,1)} %bitcast.104, bf16[197,3072]{0,1:T(8,128)(2,1)} %bitcast.106, bf16[197,768]{1,0:T(8,128)(2,1)S(1)} %copy-done.15, bf16[197,768]{1,0:T(8,128)(2,1)S(1)} %copy-done.10), kind=kOutput, calls=%fused_computation.4 | convolution fusion | flops 1867536384 | bytes 7744512 | tf_op jit(solution)/shard_map/dot_general | solution.py:33
  182.0 3.8 %convolution_convert_fusion = bf16[768,3072]{1,0:T(8,128)(2,1)} fusion(bf16[197,3072]{1,0:T(8,128)(2,1)S(1)} %copy-done.12, f32[197,768]{1,0:T(8,128)S(1)} %get-tuple-element.71, f32[768]{0:T(1024)S(1)} %copy-done.17, f32[768]{0:T(1024)S(1)} %copy-done.16, f32[197]{0:T(256)S(1)} %copy-done.22, f32[197]{0:T(256)S(1)} %broadcast_multiply_fusion), kind=kOutput, calls=%fused_computation.2 | convolution fusion | flops 932678400 | bytes 6541864 | tf_op jit(solution)/shard_map/dot_general | solution.py:33
  185.9 1.4 convolution_convert_fusion.1
  187.3 82.1 %shard_map.297 = (f32[3,96,768]{2,1,0:T(8,128)S(1)}, f32[12,768]{1,0:T(8,128)S(1)}) custom-call(bf16[8,96,3072]{2,1,0:T(8,128)(2,1)S(1)} %bitcast.87, bf16[8,96,3072]{2,1,0:T(8,128)(2,1)} %bitcast.88, bf16[8,96,3072]{2,1,0:T(8,128)(2,1)} %bitcast.98, f32[12,768]{1,0:T(8,128)S(1)} %reshape.262.refs_3_), custom_call_target="tpu_custom_call" | custom-call | tf_op jit(solution)/shard_map/pallas_call | solution.py:431
  273.1 4.8 %fusion.34 = bf16[197,768]{1,0:T(8,128)(2,1)} fusion(f32[197,768]{1,0:T(8,128)S(1)} %get-tuple-element.71, bf16[197,3072]{1,0:T(8,128)(2,1)S(1)} %copy-done.1, bf16[768,3072]{1,0:T(8,128)(2,1)} %bitcast.122, f32[768]{0:T(1024)S(1)} %copy-done.33), kind=kOutput, calls=%fused_computation.50 | convolution fusion | flops 930016512 | bytes 6839808 | tf_op jit(solution)/shard_map/dot_general | solution.py:39
  (126 shorter events, 12.0 us)
Async XLA Ops:
  3.0 112.2 %copy-start.24 = (f32[197]{0:T(256)}, f32[197]{0:T(256)S(1)}, u32[]{:S(2)}) copy-start(f32[197]{0:T(256)S(1)} %fusion.44) | copy-start | bytes 2368
  4.2 111.0 %copy-start.9 = (bf16[197,768]{1,0:T(8,128)(2,1)}, bf16[197,768]{1,0:T(8,128)(2,1)S(1)}, u32[]{:S(2)}) copy-start(bf16[197,768]{1,0:T(8,128)(2,1)S(1)} %fusion.42) | copy-start | bytes 907780
  119.1 5.4 %copy-start.6 = (bf16[197,4,1,192]{0,3,2,1:T(8,128)(2,1)}, bf16[197,4,1,192]{0,3,2,1:T(8,128)(2,1)S(1)}, u32[]{:S(2)}) copy-start(bf16[197,4,1,192]{0,3,2,1:T(8,128)(2,1)S(1)} %slice.112) | copy-start | bytes 907780
  124.9 4.8 %copy-start.4 = (bf16[1,4,4,3,197,64]{4,5,3,2,1,0:T(8,128)(2,1)}, bf16[1,4,4,3,197,64]{4,5,3,2,1,0:T(8,128)(2,1)S(1)}, u32[]{:S(2)}) copy-start(bf16[1,4,4,3,197,64]{4,5,3,2,1,0:T(8,128)(2,1)S(1)} %pad_maximum_fusion) | copy-start | bytes 3631108
  125.5 4.4 %copy-start.16 = (f32[768]{0:T(1024)S(1)}, f32[768]{0:T(1024)}, u32[]{:S(2)}) copy-start(f32[768]{0:T(1024)} %param.28) | copy-start | bytes 9220
  125.5 4.4 %copy-start.17 = (f32[768]{0:T(1024)S(1)}, f32[768]{0:T(1024)}, u32[]{:S(2)}) copy-start(f32[768]{0:T(1024)} %param.29) | copy-start | bytes 9220
  129.9 13.9 %copy-start.21 = (f32[197]{0:T(256)}, f32[197]{0:T(256)S(1)}, u32[]{:S(2)}) copy-start(f32[197]{0:T(256)S(1)} %fusion.60) | copy-start | bytes 2368
  130.0 8.8 %copy-start.2 = (bf16[197,768]{1,0:T(8,128)(2,1)S(1)}, bf16[197,768]{1,0:T(8,128)(2,1)}, u32[]{:S(2)}) copy-start(bf16[197,768]{1,0:T(8,128)(2,1)} %param.18) | copy-start | bytes 907780
  143.8 5.3 %copy-start.11 = (bf16[197,3072]{1,0:T(8,128)(2,1)}, bf16[197,3072]{1,0:T(8,128)(2,1)S(1)}, u32[]{:S(2)}) copy-start(bf16[197,3072]{1,0:T(8,128)(2,1)S(1)} %get-tuple-element.80) | copy-start | bytes 3631108
  143.8 7.1 %slice-start = ((s8[4718592]{0:T(1024)(128)(4,1)}), s8[4194304]{0:T(1024)(128)(4,1)S(1)}, s32[]{:S(2)}) async-start(s8[4718592]{0:T(1024)(128)(4,1)} %bitcast.90), calls=%async_computation | async-start | bytes 8388608
  143.8 7.1 %slice-start.1 = ((s8[4718592]{0:T(1024)(128)(4,1)}), s8[524288]{0:T(1024)(128)(4,1)S(1)}, s32[]{:S(2)}) async-start(s8[4718592]{0:T(1024)(128)(4,1)} %bitcast.90), calls=%async_computation.1 | async-start | bytes 1048576
  160.9 5.6 %copy-start.8 = (bf16[197,4,1,192]{0,3,2,1:T(8,128)(2,1)S(1)}, bf16[197,4,1,192]{0,3,2,1:T(8,128)(2,1)}, u32[]{:S(2)}) copy-start(bf16[197,4,1,192]{0,3,2,1:T(8,128)(2,1)} %copy-done.7) | copy-start | bytes 907780
  166.5 3.5 %slice-start.2 = ((s8[4718592]{0:T(1024)(128)(4,1)}), s8[4194304]{0:T(1024)(128)(4,1)S(1)}, s32[]{:S(2)}) async-start(s8[4718592]{0:T(1024)(128)(4,1)} %bitcast.95), calls=%async_computation.2 | async-start | bytes 8388608
  166.5 3.1 %copy-start.13 = (bf16[12,197,64]{1,2,0:T(8,128)(2,1)S(1)}, bf16[12,197,64]{1,2,0:T(8,128)(2,1)}, u32[]{:S(2)}) copy-start(bf16[12,197,64]{1,2,0:T(8,128)(2,1)} %fusion.26) | copy-start | bytes 907780
  166.5 3.5 %slice-start.3 = ((s8[4718592]{0:T(1024)(128)(4,1)}), s8[524288]{0:T(1024)(128)(4,1)S(1)}, s32[]{:S(2)}) async-start(s8[4718592]{0:T(1024)(128)(4,1)} %bitcast.95), calls=%async_computation.3 | async-start | bytes 1048576
  170.3 2.3 copy-start.20
  170.3 2.4 copy-start.31
  170.3 2.4 copy-start.30
  170.3 2.4 copy-start.3
  170.3 2.4 copy-start.27
  174.1 7.9 %copy-start.12 = (bf16[197,3072]{1,0:T(8,128)(2,1)S(1)}, bf16[197,3072]{1,0:T(8,128)(2,1)}, u32[]{:S(2)}) copy-start(bf16[197,3072]{1,0:T(8,128)(2,1)} %copy-done.11) | copy-start | bytes 3631108
  174.1 7.9 %copy-start.22 = (f32[197]{0:T(256)S(1)}, f32[197]{0:T(256)}, u32[]{:S(2)}) copy-start(f32[197]{0:T(256)} %copy-done.21) | copy-start | bytes 2368
  182.0 3.8 %copy-start.1 = (bf16[197,3072]{1,0:T(8,128)(2,1)S(1)}, bf16[197,3072]{1,0:T(8,128)(2,1)}, u32[]{:S(2)}) copy-start(bf16[197,3072]{1,0:T(8,128)(2,1)} %get-tuple-element.46) | copy-start | bytes 3631108
  187.3 85.8 %copy-start.33 = (f32[768]{0:T(1024)S(1)}, f32[768]{0:T(1024)}, u32[]{:S(2)}) copy-start(f32[768]{0:T(1024)} %param.33) | copy-start | bytes 9220
  (14 other events, 19.9 us)

commit v3 on v2

--- a/solution.py
+++ b/solution.py
@@ -480,7 +480,7 @@
     rows, local = w_query.shape
     heads = width // HEAD_DIM
     scale = HEAD_DIM ** (-0.5)
-    head_shape = (images, SEQ, heads, HEAD_DIM)
+    head_shape = (images, heads, SEQ, HEAD_DIM)
     attn_shard = jnp.concatenate([w_query, w_key, w_value, w_out], axis=1)
     bias = jnp.concatenate([query_bias, value_bias, up_bias])
     *weights, both = gather_weights((attn_shard, w_up, w_down), bias.reshape(-1, 128), n_dp, n_mp)
@@ -498,24 +498,28 @@
         )
         return stacked.transpose(0, 4, 1, 2, 3, 5).reshape(own_rows, -1)
 
-    def slot_of(array, slot):
-        return array.reshape(own_rows, n_mp, 4, local)[:, :, slot].reshape(own_rows, width)
+    def head_major(array):
+        array = lax.optimization_barrier(array)
+        return array.reshape(images, SEQ, n_mp, 4, near, HEAD_DIM).transpose(0, 2, 3, 4, 1, 5)
 
     inputs = tokens.astype(jnp.float32)
     normed_f, norm1_back = jax.vjp(layer_norm, inputs, ln1_gain, ln1_bias)
     normed = normed_f.astype(jnp.bfloat16)
-    projected = matmul(normed, attn)
-    queries = (slot_of(projected, 0) + query_bias).astype(jnp.bfloat16).reshape(head_shape)
-    keys_low = slot_of(projected, 1).astype(jnp.bfloat16).reshape(head_shape)
-    values_low = (slot_of(projected, 2) + value_bias).astype(jnp.bfloat16).reshape(head_shape)
+    zero_bias = jnp.zeros((n_mp, local), jnp.float32)
+    slot_bias = jnp.stack(
+        [query_bias.reshape(n_mp, local), zero_bias, value_bias.reshape(n_mp, local), zero_bias],
+        axis=1,
+    ).reshape(-1)
+    projected = head_major((matmul(normed, attn) + slot_bias).astype(jnp.bfloat16))
+    queries, keys_low, values_low = (projected[:, :, slot].reshape(head_shape) for slot in range(3))
     scaled = (
-        jnp.einsum("bqhd,bkhd->bhqk", queries, keys_low, preferred_element_type=jnp.float32) * scale
+        jnp.einsum("bhqd,bhkd->bhqk", queries, keys_low, preferred_element_type=jnp.float32) * scale
     )
     row_top = jnp.max(scaled, axis=-1, keepdims=True)
     expos = jnp.exp(scaled - row_top)
     probs = expos / jnp.sum(expos, axis=-1, keepdims=True)
     probs_low = probs.astype(jnp.bfloat16)
-    mixed = jnp.einsum("bhqk,bkhd->bhqd", probs_low, values_low, preferred_element_type=jnp.float32)
+    mixed = jnp.einsum("bhqk,bhkd->bhqd", probs_low, values_low, preferred_element_type=jnp.float32)
     mixed = mixed.astype(jnp.bfloat16)
     none = jnp.zeros_like(mixed)
     mixed_slots = interleave(none, none, none, mixed)
@@ -539,22 +543,22 @@
     grad_middle = grad_out + grad_mid_norm
     grad_branch = grad_middle.astype(jnp.bfloat16)
     out_bias_part = column_sums(grad_branch)
-    grad_mixed = slot_of(matmul(grad_branch, attn), 3).astype(jnp.bfloat16).reshape(head_shape)
+    grad_mixed = head_major(matmul(grad_branch, attn).astype(jnp.bfloat16))[:, :, 3].reshape(head_shape)
     grad_probs = jnp.einsum(
-        "bqhd,bkhd->bhqk", grad_mixed, values_low, preferred_element_type=jnp.float32
+        "bhqd,bhkd->bhqk", grad_mixed, values_low, preferred_element_type=jnp.float32
     )
     grad_values = jnp.einsum(
-        "bhqk,bqhd->bhkd", probs_low, grad_mixed, preferred_element_type=jnp.float32
+        "bhqk,bhqd->bhkd", probs_low, grad_mixed, preferred_element_type=jnp.float32
     )
     grad_values = grad_values.astype(jnp.bfloat16)
     inner = jnp.sum(probs * grad_probs, axis=-1, keepdims=True)
     grad_scores = (probs * (grad_probs - inner) * scale).astype(jnp.bfloat16)
     grad_queries = jnp.einsum(
-        "bhqk,bkhd->bhqd", grad_scores, keys_low, preferred_element_type=jnp.float32
+        "bhqk,bhkd->bhqd", grad_scores, keys_low, preferred_element_type=jnp.float32
     )
     grad_queries = grad_queries.astype(jnp.bfloat16)
     grad_keys = jnp.einsum(
-        "bhqk,bqhd->bhkd", grad_scores, queries, preferred_element_type=jnp.float32
+        "bhqk,bhqd->bhkd", grad_scores, queries, preferred_element_type=jnp.float32
     )
     grad_keys = grad_keys.astype(jnp.bfloat16)
     query_bias_part = jnp.sum(grad_queries.astype(jnp.float32), axis=(0, 2)).reshape(-1)

time: 279 us -> 269 us (0.964)
  matrix products: 69.1 us -> 64 us
  local copies, waits for them, and re-layouts: 14.8 us -> 12 us
    dot_general x1 -> x0, local copies, waits for them, and re-layouts: 6.71 us -> none  [matmul(): return jnp.dot(left, right, preferred_element_type=jnp.float32)]
    dot_general x4, matrix products: 16 us -> 12.9 us  [times_transposed(): lax.dot_general(left, right, (((1,), (1,)), ((), ())), preferred_element_...]
where the time goes in v3:
time: 269 us
  Pallas kernels  183 us (68%)
  matrix products  64 us (24%)
  local copies, waits for them, and re-layouts  12 us (4%)
  other arithmetic  8.14 us (3%)
    pallas_call x1, Pallas kernels, gather_weights(): pl.pallas_call(functools.partial(gather_kernel, n_dp, n_mp, halves, n_mat...  101 us
    pallas_call x1, Pallas kernels, reduce_gradients(): pl.pallas_call(functools.partial(reduce_kernel, n_dp, n_mp, halves, n_mat...  82.3 us
    dot_general x4, matrix products, matmul(): return jnp.dot(left, right, preferred_element_type=jnp.float32)  17.8 us
    dot_general x3, matrix products, contract_rows(): lax.dot_general(left, right, (((0,), (0,)), ((), ())), preferred_element_...  12.9 us
    dot_general x4, matrix products, times_transposed(): lax.dot_general(left, right, (((1,), (1,)), ((), ())), preferred_element_...  12.9 us
    dot_general x1, matrix products, per_device(): jnp.einsum('bhqk,bhkd->bhqd', grad_scores, keys_low, preferred_element_ty...  5.54 us

profile of v3, /device:TPU:0, one launch (start us, length us, event | category | flops | bytes accessed | tf_op | source)
XLA Modules:
  0.0 268.6 jit_solution(16067123862515335521)
XLA Ops:
  1.8 1.2 fusion.45
  3.0 1.2 fusion.43
  4.2 1.8 pad_maximum_fusion.2.refs_0_
  5.9 1.4 concatenate.16
  7.3 101.1 %shard_map.296 = (bf16[8,96,3072]{2,1,0:T(8,128)(2,1)}, bf16[8,96,3072]{2,1,0:T(8,128)(2,1)}, bf16[8,96,3072]{2,1,0:T(8,128)(2,1)}, f32[4,9,128]{2,1,0:T(8,128)}) custom-call(bf16[96,768]{1,0:T(8,128)(2,1)} %pad_maximum_fusion.2.refs_0_, bf16[96,768]{1,0:T(8,128)(2,1)} %refs_1_.1, bf16[96,768]{1,0:T(8,128)(2,1)} %refs_2_.1, f32[9,128]{1,0:T(8,128)} %bitcast.124), custom_call_target="tpu_custom_call" | custom-call | tf_op jit(solution)/shard_map/pallas_call | solution.py:212
  109.4 3.5 %fusion.2 = bf16[197,3072]{1,0:T(8,128)(2,1)S(1)} fusion(bf16[197,768]{1,0:T(8,128)(2,1)S(1)} %fusion.43, bf16[768,3072]{1,0:T(8,128)(2,1)} %bitcast.94, f32[3072]{0:T(1024)S(1)} %add.94), kind=kOutput, calls=%fused_computation.8 | convolution fusion | flops 930772992 | bytes 6243840 | tf_op jit(solution)/shard_map/dot_general | solution.py:29
  113.9 2.4 fusion.70
  116.3 2.2 convolution_convert_fusion.5
  119.7 1.7 fusion.71
  121.8 8.7 %multiply_convert_fusion.1 = (bf16[197,3072]{1,0:T(8,128)(2,1)}, f32[197,3072]{1,0:T(8,128)S(1)}, f32[197,3072]{1,0:T(8,128)S(1)}) fusion(f32[3072]{0:T(1024)S(1)} %add.103, bf16[768,3072]{1,0:T(8,128)(2,1)} %bitcast.130, f32[197,768]{1,0:T(8,128)S(1)} %get-tuple-element.72, f32[768]{0:T(1024)S(1)} %copy-done.18, f32[768]{0:T(1024)S(1)} %copy-done.17, ...), kind=kOutput, calls=%fused_computation.20 | convolution fusion | flops 970261248 | bytes 11395624 | tf_op jit(solution)/shard_map/dot_general | solution.py:29
  130.5 4.5 %convert_reduce_fusion = (f32[3072]{0:T(1024)S(1)}, bf16[197,3072]{1,0:T(8,128)(2,1)S(1)}) fusion(f32[197,3072]{1,0:T(8,128)S(1)} %get-tuple-element.47, f32[197,3072]{1,0:T(8,128)S(1)} %get-tuple-element.73, bf16[768,3072]{1,0:T(8,128)(2,1)} %bitcast.128, bf16[197,768]{1,0:T(8,128)(2,1)S(1)} %copy-done.2), kind=kOutput, calls=%fused_computation.15 | convolution fusion | flops 939242496 | bytes 11085312 | tf_op jit(solution)/shard_map/dot_general | solution.py:29
  135.0 4.6 %multiply_reduce_fusion.2 = (f32[768]{0:T(1024)S(1)}, f32[197]{0:T(256)S(1)}, f32[768]{0:T(1024)S(1)}, f32[197,768]{1,0:T(8,128)S(1)}) fusion(f32[197,768]{1,0:T(8,128)S(1)} %get-tuple-element.72, f32[197]{0:T(256)S(1)} %fusion.56, f32[197]{0:T(256)S(1)} %broadcast_multiply_fusion, f32[768]{0:T(1024)S(1)} %copy-done.17, ...), kind=kOutput, calls=%fused_computation.76 | convolution fusion | flops 930771264 | bytes 7150908 | tf_op jit(solution)/shard_map/dot_general | solution.py:39
  140.9 1.2 convolution_convert_fusion.3
  142.1 1.6 copy.48
  144.8 2.9 %fusion.74 = f32[12,197,197]{1,2,0:T(8,128)} fusion(bf16[12,197,64]{1,2,0:T(8,128)(2,1)S(1)} %bitcast.112, bf16[12,197,64]{1,2,0:T(8,128)(2,1)} %bitcast.107), kind=kOutput, calls=%fused_computation.137 | convolution fusion | flops 59610624 | bytes 2468016 | tf_op jit(solution)/shard_map/bhqd,bhkd->bhqk/dot_general | solution.py:547
  147.7 5.5 %convert_reduce_fusion.3 = (f32[12,64]{1,0:T(8,128)S(1)}, bf16[12,197,64]{1,2,0:T(8,128)(2,1)}) fusion(bf16[12,197,64]{1,2,0:T(8,128)(2,1)S(1)} %bitcast.117, f32[12,197,197]{1,2,0:T(8,128)} %fusion.74, f32[12,197,197]{1,2,0:T(8,128)} %get-tuple-element.70, f32[12,197]{1,0:T(8,128)S(1)} %get-tuple-element.69), kind=kOutput, calls=%fused_computation.63 | convolution fusion | flops 63326260 | bytes 4343376 | tf_op jit(solution)/shard_map/bhqk,bhkd->bhqd/dot_general | solution.py:556
  153.2 4.8 %fusion.27 = bf16[12,197,64]{1,2,0:T(8,128)(2,1)S(1)} fusion(bf16[12,197,64]{1,2,0:T(8,128)(2,1)S(1)} %bitcast.115, f32[12,197,197]{1,2,0:T(8,128)} %fusion.74, f32[12,197,197]{1,2,0:T(8,128)} %get-tuple-element.70, f32[12,197]{1,0:T(8,128)S(1)} %get-tuple-element.69), kind=kOutput, calls=%fused_computation.42 | convolution fusion | flops 63024436 | bytes 4340304 | tf_op jit(solution)/shard_map/bhqk,bhqd->bhkd/dot_general | solution.py:560
  158.0 2.5 convert_reduce_fusion.2
  161.4 1.8 fusion.64
  165.0 7.7 %convolution_convert_fusion.2 = bf16[768,3072]{1,0:T(8,128)(2,1)} fusion(bf16[197,3072]{0,1:T(8,128)(2,1)} %bitcast.109, bf16[197,3072]{0,1:T(8,128)(2,1)} %bitcast.111, bf16[197,768]{1,0:T(8,128)(2,1)S(1)} %copy-done.7, bf16[197,768]{1,0:T(8,128)(2,1)S(1)} %copy-done.16), kind=kOutput, calls=%fused_computation.4 | convolution fusion | flops 1867536384 | bytes 7744512 | tf_op jit(solution)/shard_map/dot_general | solution.py:33
  172.7 3.8 %convolution_convert_fusion = bf16[768,3072]{1,0:T(8,128)(2,1)} fusion(bf16[197,3072]{1,0:T(8,128)(2,1)S(1)} %copy-done.9, f32[197,768]{1,0:T(8,128)S(1)} %get-tuple-element.72, f32[768]{0:T(1024)S(1)} %copy-done.18, f32[768]{0:T(1024)S(1)} %copy-done.17, f32[197]{0:T(256)S(1)} %fusion.56, f32[197]{0:T(256)S(1)} %broadcast_multiply_fusion), kind=kOutput, calls=%fused_computation.2 | convolution fusion | flops 932678400 | bytes 6541864 | tf_op jit(solution)/shard_map/dot_general | solution.py:33
  176.6 1.4 convolution_convert_fusion.1
  178.0 82.3 %shard_map.297 = (f32[3,96,768]{2,1,0:T(8,128)S(1)}, f32[12,768]{1,0:T(8,128)S(1)}) custom-call(bf16[8,96,3072]{2,1,0:T(8,128)(2,1)S(1)} %bitcast.91, bf16[8,96,3072]{2,1,0:T(8,128)(2,1)} %bitcast.92, bf16[8,96,3072]{2,1,0:T(8,128)(2,1)} %bitcast.104, f32[12,768]{1,0:T(8,128)S(1)} %reshape.245.refs_3_), custom_call_target="tpu_custom_call" | custom-call | tf_op jit(solution)/shard_map/pallas_call | solution.py:431
  263.9 4.7 %fusion.35 = bf16[197,768]{1,0:T(8,128)(2,1)} fusion(f32[197,768]{1,0:T(8,128)S(1)} %get-tuple-element.72, bf16[197,3072]{1,0:T(8,128)(2,1)S(1)} %copy-done.1, bf16[768,3072]{1,0:T(8,128)(2,1)} %bitcast.129, f32[768]{0:T(1024)S(1)} %copy-done.21), kind=kOutput, calls=%fused_computation.53 | convolution fusion | flops 930016512 | bytes 6839808 | tf_op jit(solution)/shard_map/dot_general | solution.py:39
  (109 shorter events, 13.0 us)
Async XLA Ops:
  4.2 108.7 %copy-start.15 = (bf16[197,768]{1,0:T(8,128)(2,1)}, bf16[197,768]{1,0:T(8,128)(2,1)S(1)}, u32[]{:S(2)}) copy-start(bf16[197,768]{1,0:T(8,128)(2,1)S(1)} %fusion.43) | copy-start | bytes 907780
  113.9 4.7 %copy-start.3 = (bf16[1,4,1,3,197,64]{4,5,3,2,1,0:T(8,128)(2,1)}, bf16[1,4,1,3,197,64]{4,5,3,2,1,0:T(8,128)(2,1)S(1)}, u32[]{:S(2)}) copy-start(bf16[1,4,1,3,197,64]{4,5,3,2,1,0:T(8,128)(2,1)S(1)} %get-tuple-element.49) | copy-start | bytes 907780
  113.9 4.7 %copy-start.10 = (bf16[1,4,1,3,197,64]{4,5,3,2,1,0:T(8,128)(2,1)}, bf16[1,4,1,3,197,64]{4,5,3,2,1,0:T(8,128)(2,1)S(1)}, u32[]{:S(2)}) copy-start(bf16[1,4,1,3,197,64]{4,5,3,2,1,0:T(8,128)(2,1)S(1)} %get-tuple-element.50) | copy-start | bytes 907780
  113.9 4.7 %copy-start.12 = (bf16[1,4,1,3,197,64]{4,5,3,2,1,0:T(8,128)(2,1)}, bf16[1,4,1,3,197,64]{4,5,3,2,1,0:T(8,128)(2,1)S(1)}, u32[]{:S(2)}) copy-start(bf16[1,4,1,3,197,64]{4,5,3,2,1,0:T(8,128)(2,1)S(1)} %get-tuple-element.48) | copy-start | bytes 907780
  116.3 2.9 %slice-start = ((s8[4718592]{0:T(1024)(128)(4,1)}), s8[4194304]{0:T(1024)(128)(4,1)S(1)}, s32[]{:S(2)}) async-start(s8[4718592]{0:T(1024)(128)(4,1)} %bitcast.95), calls=%async_computation | async-start | bytes 8388608
  116.3 3.0 %slice-start.1 = ((s8[4718592]{0:T(1024)(128)(4,1)}), s8[524288]{0:T(1024)(128)(4,1)S(1)}, s32[]{:S(2)}) async-start(s8[4718592]{0:T(1024)(128)(4,1)} %bitcast.95), calls=%async_computation.1 | async-start | bytes 1048576
  118.9 2.6 copy-start.4
  119.7 2.0 copy-start.17
  119.7 2.0 copy-start.18
  121.8 8.7 %copy-start.2 = (bf16[197,768]{1,0:T(8,128)(2,1)S(1)}, bf16[197,768]{1,0:T(8,128)(2,1)}, u32[]{:S(2)}) copy-start(bf16[197,768]{1,0:T(8,128)(2,1)} %param.18) | copy-start | bytes 907780
  135.0 4.7 %copy-start.8 = (bf16[197,3072]{1,0:T(8,128)(2,1)}, bf16[197,3072]{1,0:T(8,128)(2,1)S(1)}, u32[]{:S(2)}) copy-start(bf16[197,3072]{1,0:T(8,128)(2,1)S(1)} %get-tuple-element.81) | copy-start | bytes 3631108
  135.0 5.9 %slice-start.2 = ((s8[4718592]{0:T(1024)(128)(4,1)}), s8[4194304]{0:T(1024)(128)(4,1)S(1)}, s32[]{:S(2)}) async-start(s8[4718592]{0:T(1024)(128)(4,1)} %bitcast.98), calls=%async_computation.2 | async-start | bytes 8388608
  135.0 5.9 %slice-start.3 = ((s8[4718592]{0:T(1024)(128)(4,1)}), s8[524288]{0:T(1024)(128)(4,1)S(1)}, s32[]{:S(2)}) async-start(s8[4718592]{0:T(1024)(128)(4,1)} %bitcast.98), calls=%async_computation.3 | async-start | bytes 1048576
  143.7 4.0 %copy-start.13 = (bf16[1,4,1,3,197,64]{4,5,3,2,1,0:T(8,128)(2,1)S(1)}, bf16[1,4,1,3,197,64]{4,5,3,2,1,0:T(8,128)(2,1)}, u32[]{:S(2)}) copy-start(bf16[1,4,1,3,197,64]{4,5,3,2,1,0:T(8,128)(2,1)} %copy-done.12) | copy-start | bytes 907780
  147.7 5.5 %copy-start.11 = (bf16[1,4,1,3,197,64]{4,5,3,2,1,0:T(8,128)(2,1)S(1)}, bf16[1,4,1,3,197,64]{4,5,3,2,1,0:T(8,128)(2,1)}, u32[]{:S(2)}) copy-start(bf16[1,4,1,3,197,64]{4,5,3,2,1,0:T(8,128)(2,1)} %copy-done.10) | copy-start | bytes 907780
  158.0 3.1 %slice-start.4 = ((s8[4718592]{0:T(1024)(128)(4,1)}), s8[4194304]{0:T(1024)(128)(4,1)S(1)}, s32[]{:S(2)}) async-start(s8[4718592]{0:T(1024)(128)(4,1)} %bitcast.101), calls=%async_computation.4 | async-start | bytes 8388608
  158.0 2.5 copy-start.14
  158.0 3.1 %slice-start.5 = ((s8[4718592]{0:T(1024)(128)(4,1)}), s8[524288]{0:T(1024)(128)(4,1)S(1)}, s32[]{:S(2)}) async-start(s8[4718592]{0:T(1024)(128)(4,1)} %bitcast.101), calls=%async_computation.5 | async-start | bytes 1048576
  160.9 2.3 copy-start.5
  163.2 1.9 copy-start.7
  163.2 1.8 copy-start.16
  165.0 7.7 %copy-start.9 = (bf16[197,3072]{1,0:T(8,128)(2,1)S(1)}, bf16[197,3072]{1,0:T(8,128)(2,1)}, u32[]{:S(2)}) copy-start(bf16[197,3072]{1,0:T(8,128)(2,1)} %copy-done.8) | copy-start | bytes 3631108
  172.7 3.8 %copy-start.1 = (bf16[197,3072]{1,0:T(8,128)(2,1)S(1)}, bf16[197,3072]{1,0:T(8,128)(2,1)}, u32[]{:S(2)}) copy-start(bf16[197,3072]{1,0:T(8,128)(2,1)} %get-tuple-element.46) | copy-start | bytes 3631108
  178.0 85.9 %copy-start.21 = (f32[768]{0:T(1024)S(1)}, f32[768]{0:T(1024)}, u32[]{:S(2)}) copy-start(f32[768]{0:T(1024)} %param.33) | copy-start | bytes 9220
  (4 other events, 3.9 us)
